TPU v7x, 256 devices: a whole 4x4x8 slice. The times are simulated.
256 devices in a mesh: segment: 2 (over core), tile: 8 (over x_lo, y), chan: 16 (over z, x_hi).
Axes of the slice: x: 4 (x_hi: 2, x_lo: 2; x = x_hi * 2 + x_lo), y: 4, z: 8, core: 2. Of those that a mesh axis runs over, the one named last changes fastest.
Arguments:
- video: bfloat16 [2, 16, 128, 256, 256], P('segment', None, ('tile', 'chan')), may hold values from -6 to 6
- spatial_weight: bfloat16 [9, 256, 256], replicated, may hold values from -0.125 to 0.125
- temporal_weight: bfloat16 [3, 256, 512], replicated, may hold values from -0.21875 to 0.21875
- latent_grad: bfloat16 [2, 8, 128, 256, 512], P('segment', 'tile', None, 'chan'), may hold values from -0.008239746 to 0.008239746
Outputs:
- latents: bfloat16 [2, 8, 128, 256, 512], P('segment', 'tile', None, 'chan')
- temporal_grad: float32 [3, 256, 512], replicated
All inputs are finite; a program needn't handle non-finite values.
Results may differ from a plain program's by a relative error of at most 0.005.
Values may be sent and summed in bfloat16 or wider, within the bound.
No kernel may reach another device: no remote copies, remote signals or barrier semaphores. Data moves between devices by JAX's collectives and lax.ppermute only.
A program may use at most 128 MiB of HBM per device.

v0:
```python
import jax
import jax.numpy as jnp
from jax import lax
from jax.sharding import PartitionSpec as P


def swapped(shard, axis, distance):
    return lax.ppermute(shard, axis, [(i, i ^ 1 << distance) for i in range(lax.axis_size(axis))])


def with_halo(block, sides, width):
    for axis, dim in sides:
        count = lax.axis_size(axis)
        forward = [(i, i + 1) for i in range(count - 1)]
        backward = [(target, source) for source, target in forward]
        low = lax.ppermute(
            lax.slice_in_dim(block, block.shape[dim] - width, None, axis=dim), axis, forward
        )
        high = lax.ppermute(lax.slice_in_dim(block, 0, width, axis=dim), axis, backward)
        block = jnp.concatenate([low, block, high], axis=dim)
    return block


def contract_rows(flat, upstream):
    return lax.dot_general(
        flat, upstream, (((0,), (0,)), ((), ())), preferred_element_type=jnp.float32
    )


def convolve(widened, spatial_weight, row_count, width):
    num_frames = widened.shape[0]
    channels = widened.shape[3]
    total = jnp.zeros((num_frames * row_count * width, channels), jnp.float32)
    for across in range(3):
        for along in range(3):
            window = widened[:, across : across + row_count, along : along + width].reshape(
                (-1, channels)
            )
            total = total + jnp.dot(
                window, spatial_weight[3 * across + along], preferred_element_type=jnp.float32
            )
    return jax.nn.silu(total).astype(jnp.bfloat16).reshape((num_frames, row_count, width, channels))


def body(video, spatial_weight, temporal_weight, latent_grad):
    frames = video[0]
    num_frames, row_count, width, channels = frames.shape
    out_channels = temporal_weight.shape[2]
    returned = swapped(latent_grad, "segment", 0)
    tiles = lax.axis_size("tile")
    chans = lax.axis_size("chan")
    rimmed = with_halo(frames, ((("tile", "chan"), 1),), 1)
    widened = jnp.pad(rimmed, ((0, 0), (0, 0), (1, 1), (0, 0)))
    activated = convolve(widened, spatial_weight, row_count, width)
    padded = jnp.concatenate(
        [jnp.zeros((2, row_count, width, channels), jnp.bfloat16), activated], axis=0
    )
    half = num_frames // 2
    latent = jnp.zeros((half * row_count * width, out_channels), jnp.float32)
    windows = []
    for offset in range(3):
        flat = padded[offset : offset + 2 * half : 2].reshape((-1, channels))
        windows.append(flat)
        latent = latent + jnp.dot(flat, temporal_weight[offset], preferred_element_type=jnp.float32)
    spatial_latent = latent.astype(jnp.bfloat16).reshape(
        (half, 1, 1, row_count, width, out_channels)
    )
    latents = lax.all_to_all(
        lax.all_to_all(spatial_latent, "tile", split_axis=0, concat_axis=1, tiled=True),
        "chan",
        split_axis=4,
        concat_axis=2,
        tiled=True,
    )
    latents = latents.reshape(returned.shape)
    segmented_grad = returned.reshape((1, tiles, chans, row_count, width // chans, out_channels))
    spatial_grad = lax.all_to_all(
        lax.all_to_all(segmented_grad, "tile", split_axis=1, concat_axis=0, tiled=True),
        "chan",
        split_axis=2,
        concat_axis=4,
        tiled=True,
    )
    upstream = spatial_grad.reshape((-1, out_channels))
    terms = [contract_rows(windows[offset], upstream) for offset in range(3)]
    partial_grad = jnp.stack(terms, axis=0)
    temporal_grad = lax.psum(partial_grad, ("segment", "tile", "chan"))
    return (latents, temporal_grad)


def solution(mesh):
    placed = (
        P("segment", None, ("tile", "chan"), None, None),
        P(),
        P(),
        P("segment", "tile", None, "chan", None),
    )
    return jax.shard_map(
        body,
        mesh=mesh,
        in_specs=placed,
        out_specs=(P("segment", "tile", None, "chan", None), P()),
        check_vma=False,
    )
```

profile of v0, /device:TPU:1, one launch (start us, length us, event | category | flops | bytes accessed | tf_op | source)
XLA Modules:
  0.0 548.4 jit_solution(6074036529004425140)
XLA Ops:
  7.2 5.6 %collective-permute-start = (bf16[16,1,256,256]{3,2,0,1:T(8,128)(2,1)}, bf16[16,1,256,256]{3,2,0,1:T(8,128)(2,1)S(1)}, u32[]{:S(2)}, u32[]{:S(2)}) collective-permute-start(bf16[16,1,256,256]{3,2,0,1:T(8,128)(2,1)} %bitcast.82), channel_id=1, source_target_pairs={{0,1},{1,2},{2,3},{3,4},{4,5},{5,6},{6,7},{7,8},{8,9},{9,10},{10,1... | collective-permute-start | bytes 6291464 | tf_op jit(solution)/shard_map/ppermute | solution.py:16
  15.1 4.4 fusion.24
  19.5 82.7 %collective-permute-done = bf16[16,1,256,256]{3,2,0,1:T(8,128)(2,1)S(1)} collective-permute-done((bf16[16,1,256,256]{3,2,0,1:T(8,128)(2,1)}, bf16[16,1,256,256]{3,2,0,1:T(8,128)(2,1)S(1)}, u32[]{:S(2)}, u32[]{:S(2)}) %collective-permute-start) | collective-permute-done | bytes 2097184 | tf_op jit(solution)/shard_map/ppermute | solution.py:16
  102.2 6.4 %collective-permute-done.1 = bf16[16,1,256,256]{3,2,0,1:T(8,128)(2,1)S(1)} collective-permute-done((bf16[16,1,256,256]{3,2,0,1:T(8,128)(2,1)}, bf16[16,1,256,256]{3,2,0,1:T(8,128)(2,1)S(1)}, u32[]{:S(2)}, u32[]{:S(2)}) %collective-permute-start.1) | collective-permute-done | bytes 2097184 | tf_op jit(solution)/shard_map/ppermute | solution.py:19
  108.5 4.2 fusion.5
  112.8 4.1 fusion.43
  116.9 2.6 fusion.17
  119.6 2.7 fusion.21
  122.3 2.6 fusion.26
  124.9 2.7 fusion.28
  127.6 2.7 fusion.32
  130.3 2.7 fusion.19
  133.0 2.7 fusion.30
  135.7 1.4 copy-done.7
  137.1 4.5 all-to-all-start.2
  141.6 11.8 %multiply_convert_fusion = bf16[4096,256]{1,0:T(8,128)(2,1)S(1)} fusion(f32[4096,256]{1,0:T(8,128)} %fusion.17, f32[4096,256]{1,0:T(8,128)} %fusion.19, f32[4096,256]{1,0:T(8,128)} %fusion.21, bf16[4096,256]{1,0:T(8,128)(2,1)S(1)} %bitcast.94, f32[4096,256]{1,0:T(8,128)} %fusion.24, f32[4096,256]{1,0:T(8,128)} %fusion.26, f32[4096,256]{1,0:T(8,128)} %fusion.28, ...), kind=kOutput, calls=%fused_computation.13 | convolution fusion | flops 550502400 | bytes 37879808 | tf_op jit(solution)/shard_map/dot_general | solution.py:39
  155.9 2.0 add_convert_fusion
  157.9 9.6 %all-to-all-done.2 = bf16[1,8,16,1,16,512]{5,4,2,3,0,1:T(8,128)(2,1)} async-done(((bf16[1,8,16,1,16,512]{5,4,2,3,0,1:T(8,128)(2,1)}), bf16[1,8,16,1,16,512]{5,4,2,3,0,1:T(8,128)(2,1)}, u32[]{:S(2)}, u32[]{:S(2)}) %all-to-all-start.2) | async-done | bytes 2097184 | tf_op jit(solution)/shard_map/all_to_all | solution.py:78
  167.6 3.7 all-to-all-start
  171.2 3.1 copy.12
  174.4 23.0 %all-to-all-done = bf16[8,1,1,1,256,512]{5,4,3,2,1,0:T(8,128)(2,1)S(1)} async-done(((bf16[8,1,1,1,256,512]{5,4,3,2,1,0:T(8,128)(2,1)}), bf16[8,1,1,1,256,512]{5,4,3,2,1,0:T(8,128)(2,1)S(1)}, u32[]{:S(2)}, u32[]{:S(2)}) %all-to-all-start) | async-done | bytes 2097184 | tf_op jit(solution)/shard_map/all_to_all | solution.py:69
  197.4 1.3 copy-done.2
  198.7 6.9 %all-to-all-start.3 = ((bf16[8,1,16,1,16,512]{5,4,0,3,1,2:T(8,128)(2,1)}), bf16[8,1,16,1,16,512]{5,4,0,3,1,2:T(8,128)(2,1)S(1)}, u32[]{:S(2)}, u32[]{:S(2)}) async-start(bf16[8,1,16,1,16,512]{5,4,0,3,1,2:T(8,128)(2,1)} %copy.12), calls=%async_computation.3 | async-start | bytes 4194304 | tf_op jit(solution)/shard_map/all_to_all | solution.py:77
  205.6 4.1 copy.10
  209.7 45.5 %all-to-all-done.3 = bf16[8,1,16,1,16,512]{5,4,0,3,1,2:T(8,128)(2,1)S(1)} async-done(((bf16[8,1,16,1,16,512]{5,4,0,3,1,2:T(8,128)(2,1)}), bf16[8,1,16,1,16,512]{5,4,0,3,1,2:T(8,128)(2,1)S(1)}, u32[]{:S(2)}, u32[]{:S(2)}) %all-to-all-start.3) | async-done | bytes 2097184 | tf_op jit(solution)/shard_map/all_to_all | solution.py:77
  255.2 1.3 copy-done.1
  256.5 6.0 %all-to-all-start.1 = ((bf16[1,8,1,1,256,512]{5,1,3,2,0,4:T(8,128)(2,1)}), bf16[1,8,1,1,256,512]{5,1,3,2,0,4:T(8,128)(2,1)S(1)}, u32[]{:S(2)}, u32[]{:S(2)}) async-start(bf16[1,8,1,1,256,512]{5,1,3,2,0,4:T(8,128)(2,1)} %copy.10), calls=%async_computation.1 | async-start | bytes 4194304 | tf_op jit(solution)/shard_map/all_to_all | solution.py:68
  262.6 1.9 copy.13
  268.5 45.5 %all-to-all-done.1 = bf16[1,8,1,1,256,512]{5,1,3,2,0,4:T(8,128)(2,1)S(1)} async-done(((bf16[1,8,1,1,256,512]{5,1,3,2,0,4:T(8,128)(2,1)}), bf16[1,8,1,1,256,512]{5,1,3,2,0,4:T(8,128)(2,1)S(1)}, u32[]{:S(2)}, u32[]{:S(2)}) %all-to-all-start.1) | async-done | bytes 2097184 | tf_op jit(solution)/shard_map/all_to_all | solution.py:68
  314.0 2.0 copy.11
  316.0 222.9 %all-reduce.4.cloned.1.call-done = f32[3,256,512]{2,1,0:T(8,128)} async-done(((f32[3,256,512]{2,1,0:T(8,128)}), f32[3,256,512]{2,1,0:T(8,128)}) %all-reduce.4.cloned.1.call-update) | async-done | bytes 1572880 | tf_op jit(solution)/shard_map/psum | solution.py:87
  538.8 2.7 copy.15
  (29 shorter events, 8.8 us)
Async XLA Ops:
  7.2 95.0 %collective-permute-start = (bf16[16,1,256,256]{3,2,0,1:T(8,128)(2,1)}, bf16[16,1,256,256]{3,2,0,1:T(8,128)(2,1)S(1)}, u32[]{:S(2)}, u32[]{:S(2)}) collective-permute-start(bf16[16,1,256,256]{3,2,0,1:T(8,128)(2,1)} %bitcast.82), channel_id=1, source_target_pairs={{0,1},{1,2},{2,3},{3,4},{4,5},{5,6},{6,7},{7,8},{8,9},{9,10},{10,1... | collective-permute-start | bytes 6291464 | tf_op jit(solution)/shard_map/ppermute | solution.py:16
  12.8 95.8 %collective-permute-start.1 = (bf16[16,1,256,256]{3,2,0,1:T(8,128)(2,1)}, bf16[16,1,256,256]{3,2,0,1:T(8,128)(2,1)S(1)}, u32[]{:S(2)}, u32[]{:S(2)}) collective-permute-start(bf16[16,1,256,256]{3,2,0,1:T(8,128)(2,1)} %bitcast.83), channel_id=1, source_target_pairs={{1,0},{2,1},{3,2},{4,3},{5,4},{6,5},{7,6},{8,7},{9,8},{10,9},{11,1... | collective-permute-start | bytes 6291464 | tf_op jit(solution)/shard_map/ppermute | solution.py:19
  14.1 121.6 %collective-permute-start.2 = (bf16[1,1,128,16,512]{4,3,2,1,0:T(8,128)(2,1)}, bf16[1,1,128,16,512]{4,3,2,1,0:T(8,128)(2,1)S(1)}, u32[]{:S(2)}, u32[]{:S(2)}) collective-permute-start(bf16[1,1,128,16,512]{4,3,2,1,0:T(8,128)(2,1)} %param.7), channel_id=1, source_target_pairs={{0,128},{128,0},{1,129},{129,1},{2,130},{130,2},{3,131},{131,3},{4... | collective-permute-start | bytes 6291464 | tf_op jit(solution)/shard_map/ppermute | solution.py:8
  15.1 93.4 %copy-start = (bf16[1,16,1,256,256]{4,3,2,1,0:T(8,128)(2,1)S(1)}, bf16[1,16,1,256,256]{4,3,2,1,0:T(8,128)(2,1)}, u32[]{:S(2)}) copy-start(bf16[1,16,1,256,256]{4,3,2,1,0:T(8,128)(2,1)} %param.4) | copy-start | bytes 6291460
  112.8 4.2 copy-start.8
  135.7 1.4 copy-start.7
  137.1 30.5 %all-to-all-start.2 = ((bf16[1,8,16,1,16,512]{5,4,2,3,0,1:T(8,128)(2,1)}), bf16[1,8,16,1,16,512]{5,4,2,3,0,1:T(8,128)(2,1)}, u32[]{:S(2)}, u32[]{:S(2)}) async-start(bf16[1,8,16,1,16,512]{5,4,2,3,0,1:T(8,128)(2,1)} %bitcast.103), calls=%async_computation.2 | async-start | bytes 4194304 | tf_op jit(solution)/shard_map/all_to_all | solution.py:78
  153.4 1.1 copy-start.9
  153.7 1.5 copy-start.3
  153.7 2.2 copy-start.5
  167.6 29.9 %all-to-all-start = ((bf16[8,1,1,1,256,512]{5,4,3,2,1,0:T(8,128)(2,1)}), bf16[8,1,1,1,256,512]{5,4,3,2,1,0:T(8,128)(2,1)S(1)}, u32[]{:S(2)}, u32[]{:S(2)}) async-start(bf16[8,1,1,1,256,512]{5,4,3,2,1,0:T(8,128)(2,1)} %bitcast.96), calls=%async_computation | async-start | bytes 4194304 | tf_op jit(solution)/shard_map/all_to_all | solution.py:69
  197.4 1.3 copy-start.2
  198.7 56.5 %all-to-all-start.3 = ((bf16[8,1,16,1,16,512]{5,4,0,3,1,2:T(8,128)(2,1)}), bf16[8,1,16,1,16,512]{5,4,0,3,1,2:T(8,128)(2,1)S(1)}, u32[]{:S(2)}, u32[]{:S(2)}) async-start(bf16[8,1,16,1,16,512]{5,4,0,3,1,2:T(8,128)(2,1)} %copy.12), calls=%async_computation.3 | async-start | bytes 4194304 | tf_op jit(solution)/shard_map/all_to_all | solution.py:77
  255.2 1.3 copy-start.1
  256.5 57.5 %all-to-all-start.1 = ((bf16[1,8,1,1,256,512]{5,1,3,2,0,4:T(8,128)(2,1)}), bf16[1,8,1,1,256,512]{5,1,3,2,0,4:T(8,128)(2,1)S(1)}, u32[]{:S(2)}, u32[]{:S(2)}) async-start(bf16[1,8,1,1,256,512]{5,1,3,2,0,4:T(8,128)(2,1)} %copy.10), calls=%async_computation.1 | async-start | bytes 4194304 | tf_op jit(solution)/shard_map/all_to_all | solution.py:68
  262.6 276.3 %all-reduce.4.cloned.1.call-start = ((), (), s32[]{:S(2)}) async-start(), calls=%async_computation.4 | async-start | bytes 3145728 | tf_op jit(solution)/shard_map/psum | solution.py:87
  262.6 1.9 copy-start.6
  264.5 1.2 copy-start.4
Sparse Core Ops, SparseCore 0:
  269.3 269.4 all-reduce.3
where the time goes:
time: 550 us; the launch traced here: 548 us
  waiting for transfers between devices  436 us (79%)
  matrix products  40.5 us (7%)
  starting transfers between devices  29.1 us (5%)
  local copies, waits for them, and re-layouts  23.5 us (4%)
  between operations  14.2 us (3%)
    psum x1, waiting for transfers between devices, body(): temporal_grad = lax.psum(partial_grad, ('segment', 'tile', 'chan'))  223 us
    ppermute x1, waiting for transfers between devices, with_halo(): lax.ppermute(lax.slice_in_dim(block, block.shape[dim] - width, None, axis...  82.7 us
    all_to_all x1, waiting for transfers between devices, body(): lax.all_to_all(lax.all_to_all(segmented_grad, 'tile', split_axis=1, conca...  45.5 us
    all_to_all x1, waiting for transfers between devices, body(): lax.all_to_all(lax.all_to_all(spatial_latent, 'tile', split_axis=0, conca...  45.5 us
    dot_general x9, matrix products, convolve(): jnp.dot(window, spatial_weight[3 * across + along], preferred_element_typ...  34.9 us
    all_to_all x1, waiting for transfers between devices, body(): lax.all_to_all(spatial_latent, 'tile', split_axis=0, concat_axis=1, tiled...  23 us
  transfers between devices with their start and end apart: 8, of which 7 were waited for; matrix products, arithmetic and copies ran while one was open for 11% of the time, Pallas kernels for 0%

commit v1 on v0

v1 whole, which is shorter than its diff:
```python
import jax
import jax.numpy as jnp
from jax import lax
from jax.sharding import PartitionSpec as P

GROUP = ("tile", "chan")


def exchange(pieces):
    return lax.all_to_all(pieces, GROUP, split_axis=0, concat_axis=0, tiled=True)


def other_core(shard):
    return lax.ppermute(shard, "segment", [(0, 1), (1, 0)])


def column_windows(frames, chans):
    num, width, channels = frames.shape
    blocks = frames.reshape((num, chans, width // chans, channels))
    blank = jnp.zeros((num, 1, 1, channels), frames.dtype)
    left = jnp.concatenate([blank, blocks[:, :-1, -1:]], axis=1)
    right = jnp.concatenate([blocks[:, 1:, :1], blank], axis=1)
    return jnp.concatenate([left, blocks, right], axis=2)


def activate(columns, spatial_weight):
    channels = columns.shape[2]
    pre = lax.conv_general_dilated(
        columns[None],
        spatial_weight.reshape((3, 3, channels, channels)),
        (1, 1),
        ((1, 1), (0, 0)),
        dimension_numbers=("NHWC", "HWIO", "NHWC"),
        preferred_element_type=jnp.float32,
    )
    return jax.nn.silu(pre).astype(jnp.bfloat16).reshape((-1, channels))


def contract_rows(flat, upstream):
    return lax.dot_general(
        flat, upstream, (((0,), (0,)), ((), ())), preferred_element_type=jnp.float32
    )


def summed(partial, devices):
    side = lax.axis_index("segment")
    flat = partial.reshape((2, devices, -1, 128))
    mine = lax.dynamic_index_in_dim(flat, side, 0, keepdims=False)
    sent = lax.dynamic_index_in_dim(flat, 1 - side, 0, keepdims=False)
    pair = mine + other_core(sent)
    piece = jnp.sum(exchange(pair), axis=0).astype(jnp.bfloat16)
    whole = exchange(jnp.broadcast_to(piece[None], (devices, *piece.shape)))
    away = other_core(whole)
    low = jnp.where(side == 0, whole, away)
    high = jnp.where(side == 0, away, whole)
    return jnp.stack([low, high]).astype(jnp.float32).reshape(partial.shape)


def body(video, spatial_weight, temporal_weight, latent_grad):
    tiles, chans = lax.axis_size("tile"), lax.axis_size("chan")
    devices = tiles * chans
    frames = video[0, :, 0]
    channels = frames.shape[2]
    upstream = other_core(latent_grad)
    flat_up = upstream.reshape((-1, upstream.shape[4]))
    windows = column_windows(frames, chans)
    even = windows[0::2].reshape((devices, -1, channels))
    odd = jnp.concatenate([windows[-1:], windows[1:-1:2]]).reshape((devices, -1, channels))
    even_cols = exchange(even)
    odd_cols = exchange(odd)
    newest = activate(even_cols, spatial_weight)
    oldest = lax.ppermute(newest, "tile", [(i, i + 1) for i in range(tiles - 1)])
    middle = activate(odd_cols, spatial_weight)
    middle = jnp.where(lax.axis_index("tile") > 0, middle, jnp.zeros_like(middle))
    taps = (oldest, middle, newest)
    latent = sum(
        jnp.dot(tap, temporal_weight[k], preferred_element_type=jnp.float32)
        for k, tap in enumerate(taps)
    )
    latents = latent.astype(jnp.bfloat16).reshape(upstream.shape)
    partial = jnp.stack([contract_rows(tap, flat_up) for tap in taps])
    return (latents, summed(partial, devices))


def solution(mesh):
    placed = (
        P("segment", None, ("tile", "chan"), None, None),
        P(),
        P(),
        P("segment", "tile", None, "chan", None),
    )
    return jax.shard_map(
        body,
        mesh=mesh,
        in_specs=placed,
        out_specs=(P("segment", "tile", None, "chan", None), P()),
        check_vma=False,
    )
```

time: 550 us -> 232 us (0.42)
  waiting for transfers between devices: 436 us -> 88.6 us
  blocking collectives: 0 us -> 40.8 us
  starting transfers between devices: 29.1 us -> 48.7 us
  between operations: 14.2 us -> 1 us
  matrix products: 40.5 us -> 27.8 us
  local copies, waits for them, and re-layouts: 23.5 us -> 17.8 us
    psum x1 -> x0, waiting for transfers between devices: 223 us -> none  [body(): temporal_grad = lax.psum(partial_grad, ('segment', 'tile', 'chan'))]
    ppermute x3 -> x4, waiting for transfers between devices: 89 us -> 10.2 us  [the longest x1 8.32 us: body(): lax.ppermute(newest, 'tile', [(i, i + 1) for i in range(tiles - 1)])]
    all_to_all x4 -> x3, waiting for transfers between devices: 124 us -> 78.3 us  [exchange(): lax.all_to_all(pieces, GROUP, split_axis=0, concat_axis=0, tiled=True)]
    all_to_all x0 -> x1, blocking collectives: none -> 40.8 us  [exchange(): lax.all_to_all(pieces, GROUP, split_axis=0, concat_axis=0, tiled=True)]
    dot_general x12 -> x3, matrix products: 38.3 us -> 11.9 us  [body(): jnp.dot(tap, temporal_weight[k], preferred_element_type=jnp.float32)]
    all_to_all x4 -> x3, starting transfers between devices: 21.1 us -> 37.3 us  [exchange(): lax.all_to_all(pieces, GROUP, split_axis=0, concat_axis=0, tiled=True)]
    all_to_all x4 -> x2, local copies, waits for them, and re-layouts: 11.1 us -> 1.92 us  [exchange(): lax.all_to_all(pieces, GROUP, split_axis=0, concat_axis=0, tiled=True)]
    conv_general_dilated x0 -> x2, matrix products: none -> 8.24 us  [activate(): lax.conv_general_dilated(columns[None], spatial_weight.reshape((3, 3, cha...]
  transfers between devices with their start and end apart: 8 -> 7, of which waited for: 7 -> 5; matrix products, arithmetic and copies ran while one was open for 11% -> 15% of each run, Pallas kernels for 0% -> 0%
where the time goes in v1:
time: 232 us
  waiting for transfers between devices  88.6 us (38%)
  starting transfers between devices  48.7 us (21%)
  blocking collectives  40.8 us (18%)
  matrix products  27.8 us (12%)
  local copies, waits for them, and re-layouts  17.8 us (8%)
  other arithmetic  7.06 us (3%)
    all_to_all x3, waiting for transfers between devices, exchange(): lax.all_to_all(pieces, GROUP, split_axis=0, concat_axis=0, tiled=True)  78.3 us
    all_to_all x1, blocking collectives, exchange(): lax.all_to_all(pieces, GROUP, split_axis=0, concat_axis=0, tiled=True)  40.8 us
    all_to_all x3, starting transfers between devices, exchange(): lax.all_to_all(pieces, GROUP, split_axis=0, concat_axis=0, tiled=True)  37.3 us
    dot_general x3, matrix products, body(): jnp.dot(tap, temporal_weight[k], preferred_element_type=jnp.float32)  11.9 us
    ppermute x3, starting transfers between devices, other_core(): return lax.ppermute(shard, 'segment', [(0, 1), (1, 0)])  9.79 us
    ppermute x1, waiting for transfers between devices, body(): lax.ppermute(newest, 'tile', [(i, i + 1) for i in range(tiles - 1)])  8.32 us
    conv_general_dilated x2, matrix products, activate(): lax.conv_general_dilated(columns[None], spatial_weight.reshape((3, 3, cha...  8.24 us
    dot_general x3, matrix products, contract_rows(): lax.dot_general(flat, upstream, (((0,), (0,)), ((), ())), preferred_eleme...  7.67 us
  transfers between devices with their start and end apart: 7, of which 5 were waited for; matrix products, arithmetic and copies ran while one was open for 15% of the time, Pallas kernels for 0%

profile of v1, /device:TPU:1, one launch (start us, length us, event | category | flops | bytes accessed | tf_op | source)
XLA Modules:
  0.0 231.7 jit_solution(17502867370312967713)
XLA Ops:
  0.6 2.0 fusion.41
  2.7 3.6 %fusion.4 = bf16[16,16,18,256]{3,2,1,0:T(8,128)(2,1)S(1)} fusion(bf16[16,15,1,256]{3,2,1,0:T(2,128)(2,1)S(1)} %get-tuple-element.5, bf16[16,15,1,256]{3,2,1,0:T(2,128)(2,1)S(1)} %get-tuple-element.4, bf16[16,16,16,256]{3,2,1,0:T(8,128)(2,1)} %bitcast.77), kind=kLoop, calls=%fused_computation.8 | loop fusion | flops 11796480 | bytes 4702208 | tf_op jit(solution)/shard_map/concatenate | solution.py:23
  6.3 1.6 copy-done.2
  7.9 1.2 slice.26
  9.2 16.5 %all-to-all-start = ((bf16[128,18,256]{2,1,0:T(8,128)(2,1)}), bf16[128,18,256]{2,1,0:T(8,128)(2,1)S(1)}, u32[]{:S(2)}, u32[]{:S(2)}) async-start(bf16[128,18,256]{2,1,0:T(8,128)(2,1)} %bitcast.1), calls=%async_computation | async-start | bytes 3145728 | tf_op jit(solution)/shard_map/all_to_all | solution.py:10
  25.7 1.4 slice.29
  27.1 1.3 pad_maximum_fusion
  28.4 35.2 %all-to-all-done = bf16[128,18,256]{2,1,0:T(8,128)(2,1)S(1)} async-done(((bf16[128,18,256]{2,1,0:T(8,128)(2,1)}), bf16[128,18,256]{2,1,0:T(8,128)(2,1)S(1)}, u32[]{:S(2)}, u32[]{:S(2)}) %all-to-all-start) | async-done | bytes 1179680 | tf_op jit(solution)/shard_map/all_to_all | solution.py:10
  63.6 11.0 %all-to-all-start.1 = ((bf16[128,18,256]{2,1,0:T(8,128)(2,1)}), bf16[128,18,256]{2,1,0:T(8,128)(2,1)}, u32[]{:S(2)}, u32[]{:S(2)}) async-start(bf16[128,18,256]{2,1,0:T(8,128)(2,1)} %bitcast.9), calls=%async_computation.1 | async-start | bytes 3145728 | tf_op jit(solution)/shard_map/all_to_all | solution.py:10
  74.6 1.8 collective-permute-start.1
  76.8 0.9 copy.50
  77.7 34.2 %all-to-all-done.1 = bf16[128,18,256]{2,1,0:T(8,128)(2,1)} async-done(((bf16[128,18,256]{2,1,0:T(8,128)(2,1)}), bf16[128,18,256]{2,1,0:T(8,128)(2,1)}, u32[]{:S(2)}, u32[]{:S(2)}) %all-to-all-start.1) | async-done | bytes 1179680 | tf_op jit(solution)/shard_map/all_to_all | solution.py:10
  111.9 1.7 copy.65
  115.3 4.1 %multiply_convert_fusion.1 = bf16[128,8,3,256]{3,1,2,0:T(8,128)(2,1)S(1)} fusion(pred[8,3]{0,1:T(4,128)(4,1)S(1)} %copy-done.10, bf16[3,3,256,256]{3,2,1,0:T(8,128)(2,1)S(1)} %bitcast.63, bf16[128,1,7,2,256]{4,2,3,0,1:T(8,128)(2,1)S(1)} %slice.38, bf16[128,1,8,3,256]{4,2,3,0,1:T(8,128)(2,1)S(1)} %copy.50), kind=kOutput, calls=%fused_computation.11 | convolution fusion | flops 3617587200 | bytes 5242904 | tf_op jit(solution)/shard_map/conv_general_dilated | solution.py:28
  120.4 1.6 collective-permute-start
  122.0 4.2 %fusion.20 = bf16[128,8,3,256]{3,1,2,0:T(8,128)(2,1)S(1)} fusion(pred[]{:T(512)S(6)} %gt.3, pred[8,3]{0,1:T(4,128)(4,1)S(1)} %copy-done.10, bf16[3,3,256,256]{3,2,1,0:T(8,128)(2,1)S(1)} %bitcast.64, bf16[128,1,7,2,256]{4,2,3,0,1:T(8,128)(2,1)S(1)} %slice.41, bf16[128,1,8,3,256]{4,2,3,0,1:T(8,128)(2,1)S(1)} %copy.55), kind=kOutput, calls=%fused_computation.26 | convolution fusion | flops 3618373632 | bytes 5242905 | tf_op jit(solution)/shard_map/conv_general_dilated | solution.py:28
  127.2 2.7 %convolution_bitcast_fusion = f32[1,256,512]{2,1,0:T(8,128)S(1)} fusion(bf16[2048,256]{1,0:T(8,128)(2,1)S(1)} %bitcast.66, bf16[2048,512]{1,0:T(8,128)(2,1)} %bitcast.18), kind=kOutput, calls=%fused_computation.29 | convolution fusion | flops 536870912 | bytes 3670016 | tf_op jit(solution)/shard_map/dot_general | solution.py:40
  129.9 2.3 convolution_bitcast_fusion.1
  132.2 8.3 %collective-permute-done = bf16[2048,256]{1,0:T(8,128)(2,1)S(1)} collective-permute-done((bf16[2048,256]{1,0:T(8,128)(2,1)S(1)}, bf16[2048,256]{1,0:T(8,128)(2,1)S(1)}, u32[]{:S(2)}, u32[]{:S(2)}) %collective-permute-start) | collective-permute-done | bytes 1048608 | tf_op jit(solution)/shard_map/ppermute | solution.py:72
  140.6 2.7 %convolution_bitcast_fusion.2 = f32[1,256,512]{2,1,0:T(8,128)S(1)} fusion(bf16[2048,256]{1,0:T(8,128)(2,1)S(1)} %collective-permute-done, bf16[2048,512]{1,0:T(8,128)(2,1)} %bitcast.18), kind=kOutput, calls=%fused_computation.31 | convolution fusion | flops 536870912 | bytes 3670016 | tf_op jit(solution)/shard_map/dot_general | solution.py:40
  143.3 1.3 pad_maximum_fusion.1
  144.6 1.6 reshape.42
  146.6 4.6 %collective-permute-start.2 = (f32[128,12,128]{2,0,1:T(8,128)S(1)}, f32[128,12,128]{2,0,1:T(8,128)S(1)}, u32[]{:S(2)}, u32[]{:S(2)}) collective-permute-start(f32[128,12,128]{2,0,1:T(8,128)S(1)} %bitcast.79), channel_id=1, source_target_pairs={{0,128},{128,0},{1,129},{129,1},{2,130},{130,2},{3,131},{131,3},{4... | collective-permute-start | bytes 2359304 | tf_op jit(solution)/shard_map/ppermute | solution.py:14
  151.2 1.9 collective-permute-done.2
  153.9 40.8 %all_to_all.20 = f32[128,12,128]{2,1,0:T(8,128)S(1)} all-to-all(f32[128,12,128]{2,1,0:T(8,128)S(1)} %copy.60), channel_id=1, replica_groups=mesh['segment'=2,'tile'=8,'chan'=16] {'tile','chan'}, dimensions={0} | all-to-all | bytes 1572864 | tf_op jit(solution)/shard_map/all_to_all | solution.py:10
  195.8 9.9 %all-to-all-start.3 = ((bf16[128,12,128]{2,1,0:T(8,128)(2,1)}), bf16[128,12,128]{2,1,0:T(8,128)(2,1)S(1)}, u32[]{:S(2)}, u32[]{:S(2)}) async-start(bf16[128,12,128]{2,1,0:T(8,128)(2,1)} %broadcast_in_dim.19), calls=%async_computation.3 | async-start | bytes 1048576 | tf_op jit(solution)/shard_map/all_to_all | solution.py:10
  205.7 3.8 %fusion.29 = f32[2048,512]{1,0:T(8,128)} fusion(bf16[2048,256]{1,0:T(8,128)(2,1)S(1)} %bitcast.69, bf16[3,256,512]{2,1,0:T(8,128)(2,1)} %param.6), kind=kOutput, calls=%fused_computation.41 | convolution fusion | flops 536870912 | bytes 5505024 | tf_op jit(solution)/shard_map/dot_general | solution.py:77
  209.5 2.6 %fusion.27 = f32[2048,512]{1,0:T(8,128)} fusion(bf16[2048,256]{1,0:T(8,128)(2,1)S(1)} %bitcast.67, bf16[3,256,512]{2,1,0:T(8,128)(2,1)S(1)} %copy-done.9), kind=kOutput, calls=%fused_computation.39 | convolution fusion | flops 536870912 | bytes 5505024 | tf_op jit(solution)/shard_map/dot_general | solution.py:77
  212.1 8.9 %all-to-all-done.3 = bf16[128,12,128]{2,1,0:T(8,128)(2,1)S(1)} async-done(((bf16[128,12,128]{2,1,0:T(8,128)(2,1)}), bf16[128,12,128]{2,1,0:T(8,128)(2,1)S(1)}, u32[]{:S(2)}, u32[]{:S(2)}) %all-to-all-start.3) | async-done | bytes 393248 | tf_op jit(solution)/shard_map/all_to_all | solution.py:10
  221.1 3.4 %collective-permute-start.3 = (bf16[128,12,128]{2,1,0:T(8,128)(2,1)S(1)}, bf16[128,12,128]{2,1,0:T(8,128)(2,1)S(1)}, u32[]{:S(2)}, u32[]{:S(2)}) collective-permute-start(bf16[128,12,128]{2,1,0:T(8,128)(2,1)S(1)} %all-to-all-done.3), channel_id=1, source_target_pairs={{0,128},{128,0},{1,129},{129,1},{2,130},{130,2},{3,131},{131,3},{4... | collective-permute-start | bytes 1179656 | tf_op jit(solution)/shard_map/ppermute | solution.py:14
  224.5 5.5 %add_convert_fusion = bf16[2048,512]{1,0:T(8,128)(2,1)} fusion(f32[2048,512]{1,0:T(8,128)} %fusion.27, f32[2048,512]{1,0:T(8,128)} %fusion.29, bf16[2048,256]{1,0:T(8,128)(2,1)S(1)} %copy-done.8, bf16[3,256,512]{2,1,0:T(8,128)(2,1)S(1)} %copy-done.9), kind=kOutput, calls=%fused_computation.7 | convolution fusion | flops 540016640 | bytes 11796480 | tf_op jit(solution)/shard_map/dot_general | solution.py:77
  230.3 1.4 reshape.57
  (45 shorter events, 6.8 us)
Async XLA Ops:
  0.6 114.5 %copy-start = (bf16[9,256,256]{2,1,0:T(8,128)(2,1)S(1)}, bf16[9,256,256]{2,1,0:T(8,128)(2,1)}, u32[]{:S(2)}) copy-start(bf16[9,256,256]{2,1,0:T(8,128)(2,1)} %param.5) | copy-start | bytes 3538948
  6.3 1.6 copy-start.2
  9.2 17.9 %slice-start = ((bf16[16,16,18,256]{3,2,1,0:T(8,128)(2,1)}), bf16[1,16,18,256]{3,2,1,0:T(8,128)(2,1)S(1)}, s32[]{:S(2)}) async-start(bf16[16,16,18,256]{3,2,1,0:T(8,128)(2,1)} %copy-done.2), calls=%async_computation.4 | async-start | bytes 393216 | tf_op jit(solution)/shard_map/slice | solution.py:68
  9.2 54.4 %all-to-all-start = ((bf16[128,18,256]{2,1,0:T(8,128)(2,1)}), bf16[128,18,256]{2,1,0:T(8,128)(2,1)S(1)}, u32[]{:S(2)}, u32[]{:S(2)}) async-start(bf16[128,18,256]{2,1,0:T(8,128)(2,1)} %bitcast.1), calls=%async_computation | async-start | bytes 3145728 | tf_op jit(solution)/shard_map/all_to_all | solution.py:10
  63.6 48.3 %all-to-all-start.1 = ((bf16[128,18,256]{2,1,0:T(8,128)(2,1)}), bf16[128,18,256]{2,1,0:T(8,128)(2,1)}, u32[]{:S(2)}, u32[]{:S(2)}) async-start(bf16[128,18,256]{2,1,0:T(8,128)(2,1)} %bitcast.9), calls=%async_computation.1 | async-start | bytes 3145728 | tf_op jit(solution)/shard_map/all_to_all | solution.py:10
  74.6 52.6 %collective-permute-start.1 = (bf16[1,1,128,16,512]{4,3,2,1,0:T(8,128)(2,1)}, bf16[1,1,128,16,512]{4,3,2,1,0:T(8,128)(2,1)}, u32[]{:S(2)}, u32[]{:S(2)}) collective-permute-start(bf16[1,1,128,16,512]{4,3,2,1,0:T(8,128)(2,1)} %param.7), channel_id=1, source_target_pairs={{0,128},{128,0},{1,129},{129,1},{2,130},{130,2},{3,131},{131,3},{4... | collective-permute-start | bytes 6291464 | tf_op jit(solution)/shard_map/ppermute | solution.py:14
  114.6 0.7 copy-start.10
  120.4 6.8 %copy-start.3 = (bf16[128,1,16,256]{3,2,0,1:T(8,128)(2,1)}, bf16[128,1,16,256]{3,2,0,1:T(8,128)(2,1)S(1)}, u32[]{:S(2)}) copy-start(bf16[128,1,16,256]{3,2,0,1:T(8,128)(2,1)S(1)} %copy.52) | copy-start | bytes 3145732
  120.4 20.2 %collective-permute-start = (bf16[2048,256]{1,0:T(8,128)(2,1)S(1)}, bf16[2048,256]{1,0:T(8,128)(2,1)S(1)}, u32[]{:S(2)}, u32[]{:S(2)}) collective-permute-start(bf16[2048,256]{1,0:T(8,128)(2,1)S(1)} %bitcast.65), channel_id=1, source_target_pairs={{0,16},{16,32},{32,48},{48,64},{64,80},{80,96},{96,112},{1,17},{17... | collective-permute-start | bytes 3145736 | tf_op jit(solution)/shard_map/ppermute | solution.py:72
  127.2 5.0 %copy-start.5 = (bf16[128,1,16,256]{3,2,0,1:T(8,128)(2,1)}, bf16[128,1,16,256]{3,2,0,1:T(8,128)(2,1)S(1)}, u32[]{:S(2)}) copy-start(bf16[128,1,16,256]{3,2,0,1:T(8,128)(2,1)S(1)} %copy.57) | copy-start | bytes 3145732
  140.6 2.7 %copy-start.7 = (bf16[2048,256]{1,0:T(8,128)(2,1)}, bf16[2048,256]{1,0:T(8,128)(2,1)S(1)}, u32[]{:S(2)}) copy-start(bf16[2048,256]{1,0:T(8,128)(2,1)S(1)} %collective-permute-done) | copy-start | bytes 3145732
  146.6 6.5 %collective-permute-start.2 = (f32[128,12,128]{2,0,1:T(8,128)S(1)}, f32[128,12,128]{2,0,1:T(8,128)S(1)}, u32[]{:S(2)}, u32[]{:S(2)}) collective-permute-start(f32[128,12,128]{2,0,1:T(8,128)S(1)} %bitcast.79), channel_id=1, source_target_pairs={{0,128},{128,0},{1,129},{129,1},{2,130},{130,2},{3,131},{131,3},{4... | collective-permute-start | bytes 2359304 | tf_op jit(solution)/shard_map/ppermute | solution.py:14
  153.9 51.7 %copy-start.6 = (bf16[128,1,16,256]{3,2,0,1:T(8,128)(2,1)S(1)}, bf16[128,1,16,256]{3,2,0,1:T(8,128)(2,1)}, u32[]{:S(2)}) copy-start(bf16[128,1,16,256]{3,2,0,1:T(8,128)(2,1)} %copy-done.5) | copy-start | bytes 3145732
  195.8 25.3 %all-to-all-start.3 = ((bf16[128,12,128]{2,1,0:T(8,128)(2,1)}), bf16[128,12,128]{2,1,0:T(8,128)(2,1)S(1)}, u32[]{:S(2)}, u32[]{:S(2)}) async-start(bf16[128,12,128]{2,1,0:T(8,128)(2,1)} %broadcast_in_dim.19), calls=%async_computation.3 | async-start | bytes 1048576 | tf_op jit(solution)/shard_map/all_to_all | solution.py:10
  205.7 3.8 %copy-start.4 = (bf16[128,1,16,256]{3,2,0,1:T(8,128)(2,1)S(1)}, bf16[128,1,16,256]{3,2,0,1:T(8,128)(2,1)}, u32[]{:S(2)}) copy-start(bf16[128,1,16,256]{3,2,0,1:T(8,128)(2,1)} %copy-done.3) | copy-start | bytes 3145732
  205.7 3.8 %copy-start.9 = (bf16[3,256,512]{2,1,0:T(8,128)(2,1)S(1)}, bf16[3,256,512]{2,1,0:T(8,128)(2,1)}, u32[]{:S(2)}) copy-start(bf16[3,256,512]{2,1,0:T(8,128)(2,1)} %param.6) | copy-start | bytes 2359300
  209.5 15.0 %copy-start.8 = (bf16[2048,256]{1,0:T(8,128)(2,1)S(1)}, bf16[2048,256]{1,0:T(8,128)(2,1)}, u32[]{:S(2)}) copy-start(bf16[2048,256]{1,0:T(8,128)(2,1)} %copy-done.7) | copy-start | bytes 3145732
  221.1 8.9 %collective-permute-start.3 = (bf16[128,12,128]{2,1,0:T(8,128)(2,1)S(1)}, bf16[128,12,128]{2,1,0:T(8,128)(2,1)S(1)}, u32[]{:S(2)}, u32[]{:S(2)}) collective-permute-start(bf16[128,12,128]{2,1,0:T(8,128)(2,1)S(1)} %all-to-all-done.3), channel_id=1, source_target_pairs={{0,128},{128,0},{1,129},{129,1},{2,130},{130,2},{3,131},{131,3},{4... | collective-permute-start | bytes 1179656 | tf_op jit(solution)/shard_map/ppermute | solution.py:14
  230.0 1.7 copy-start.1

commit v2 on v1

v2 whole, which is shorter than its diff:
```python
import functools

import jax
import jax.numpy as jnp
from jax import lax
from jax.experimental import pallas as pl
from jax.experimental.pallas import tpu as pltpu
from jax.sharding import PartitionSpec as P

GROUP = ("tile", "chan")
LANES = 128
COLS = 16
PIECE = 16
VMEM_BYTES = 48 * 1024 * 1024
F32 = jnp.float32
BF16 = jnp.bfloat16


def exchange(pieces):
    return lax.all_to_all(pieces, GROUP, split_axis=0, concat_axis=0, tiled=True)


def other_core(shard):
    return lax.ppermute(shard, "segment", [(0, 1), (1, 0)])


def pack_kernel(odd_ref, even_ref, out_ref):
    frames = (odd_ref[0], even_ref[0])
    blocks, height = out_ref.shape[0], out_ref.shape[1]
    place = lax.broadcasted_iota(jnp.int32, (blocks, 8, LANES), 1)
    edges = jnp.zeros((blocks, 8, LANES), F32)
    for f, frame in enumerate(frames):
        for h in range(2):
            half = frame[:, h * LANES : (h + 1) * LANES].reshape((blocks, COLS, LANES))
            start = h * 2 * COLS + f * COLS
            out_ref[:, start : start + COLS, :] = half
            wide = half.astype(F32)
            blank = jnp.zeros((1, 1, LANES), F32)
            left = jnp.concatenate([blank, wide[:-1, COLS - 1 :]], axis=0)
            right = jnp.concatenate([wide[1:, :1], blank], axis=0)
            row = h * 4 + f * 2
            edges = jnp.where(place == row, left, edges)
            edges = jnp.where(place == row + 1, right, edges)
    out_ref[:, height - 8 :, :] = edges.astype(BF16)


def pack(frames, tiles, chans):
    num, width, channels = frames.shape
    height = 4 * COLS + 8
    return pl.pallas_call(
        pack_kernel,
        grid=(tiles,),
        in_specs=[
            pl.BlockSpec((1, width, channels), lambda j: ((2 * j + num - 1) % num, 0, 0)),
            pl.BlockSpec((1, width, channels), lambda j: (2 * j, 0, 0)),
        ],
        out_specs=pl.BlockSpec((chans, height, LANES), lambda j: (j, 0, 0)),
        out_shape=jax.ShapeDtypeStruct((tiles * chans, height, LANES), BF16),
        compiler_params=pltpu.CompilerParams(vmem_limit_bytes=VMEM_BYTES),
        name="pack",
    )(frames, frames)


def silu(pre):
    return pre / (1.0 + jnp.exp(-pre))


def conv_kernel(
    rows, chunk, where_ref, y_hbm, w_hbm, u_hbm, next_hbm,
    act_ref, mine_ref, sent_ref, y_ref, w_ref, u_ref, next_ref, window_ref, grad_ref, sems,
):
    copies = [
        pltpu.make_async_copy(src, dst, sems.at[i])
        for i, (src, dst) in enumerate(
            ((y_hbm, y_ref), (w_hbm, w_ref), (u_hbm, u_ref), (next_hbm, next_ref))
        )
    ]
    for copy in copies:
        copy.start()
    channels = 2 * LANES
    side, tile = where_ref[0], where_ref[1]
    window_ref[0] = jnp.zeros(window_ref.shape[1:], BF16)
    window_ref[rows + 1] = jnp.zeros(window_ref.shape[1:], BF16)
    copies[0].wait()
    for f in (1, 0):
        for r in range(0, rows, chunk):
            place = lax.broadcasted_iota(jnp.int32, (chunk, COLS, LANES), 1)
            edges = y_ref[r : r + chunk, 4 * COLS :, :].astype(F32)
            for h in range(2):
                start = h * 2 * COLS + f * COLS
                main = y_ref[r : r + chunk, start : start + COLS, :]
                wide = main.astype(F32).reshape((chunk * COLS, LANES))
                row = h * 4 + f * 2
                shape = (chunk, COLS, LANES)
                earlier = pltpu.roll(wide, 1, 0).reshape(shape)
                later = pltpu.roll(wide, chunk * COLS - 1, 0).reshape(shape)
                earlier = jnp.where(place == 0, edges[:, row : row + 1], earlier)
                later = jnp.where(place == COLS - 1, edges[:, row + 1 : row + 2], later)
                for e, part in enumerate((earlier.astype(BF16), main, later.astype(BF16))):
                    lane = e * channels + h * LANES
                    window_ref[r + 1 : r + 1 + chunk, :, lane : lane + LANES] = part
        if f == 1:
            copies[1].wait()
        for r in range(0, rows, chunk):
            pre = jnp.zeros((chunk * COLS, channels), F32)
            for a in range(3):
                lhs = window_ref[r + a : r + a + chunk].reshape((chunk * COLS, 3 * channels))
                pre = pre + jnp.dot(lhs, w_ref[a], preferred_element_type=F32)
            value = silu(pre)
            if f == 0:
                value = jnp.where(tile > 0, value, jnp.zeros_like(value))
            act_ref[f, r * COLS : (r + chunk) * COLS, :] = value.astype(BF16)
    copies[2].wait()
    copies[3].wait()
    lanes = grad_ref.shape[1]
    blocks = u_ref.shape[1] // LANES
    for k, (f, up) in enumerate(((1, next_ref), (0, u_ref), (1, u_ref))):
        term = lax.dot_general(
            act_ref[f], up[...], (((0,), (0,)), ((), ())), preferred_element_type=F32
        )
        for g in range(channels // PIECE):
            line = k * channels + g * PIECE
            half, group = divmod(line, 3 * channels // 2)
            for b in range(blocks):
                grad_ref[half, (group // PIECE) * blocks + b] = term[
                    g * PIECE : (g + 1) * PIECE, b * LANES : (b + 1) * LANES
                ]
    mine_ref[...] = grad_ref[side]
    sent_ref[...] = grad_ref[1 - side]


def conv_and_gradient(where, pieces, spatial_weight, upstream, following):
    rows = pieces.shape[0]
    channels = spatial_weight.shape[2]
    out_channels = upstream.shape[1]
    positions = rows * COLS
    count = 3 * channels * out_channels // (2 * PIECE * LANES)
    hbm = pl.BlockSpec(memory_space=pl.ANY)
    vmem = pl.BlockSpec(memory_space=pltpu.VMEM)
    weight = spatial_weight.reshape((3, 3 * channels, channels))
    part = jax.ShapeDtypeStruct((count, PIECE, LANES), F32)
    return pl.pallas_call(
        functools.partial(conv_kernel, rows, 32),
        in_specs=[pl.BlockSpec(memory_space=pltpu.SMEM), hbm, hbm, hbm, hbm],
        out_specs=[vmem, vmem, vmem],
        out_shape=[jax.ShapeDtypeStruct((2, positions, channels), BF16), part, part],
        scratch_shapes=[
            pltpu.VMEM(pieces.shape, BF16),
            pltpu.VMEM(weight.shape, BF16),
            pltpu.VMEM(upstream.shape, BF16),
            pltpu.VMEM(following.shape, BF16),
            pltpu.VMEM((rows + 2, COLS, 3 * channels), BF16),
            pltpu.VMEM((2, count, PIECE, LANES), F32),
            pltpu.SemaphoreType.DMA((4,)),
        ],
        compiler_params=pltpu.CompilerParams(vmem_limit_bytes=VMEM_BYTES),
        cost_estimate=pl.CostEstimate(
            flops=2 * positions * (18 * channels * channels + 3 * channels * out_channels),
            bytes_accessed=10_000_000,
            transcendentals=2 * positions * channels,
        ),
        name="conv_and_gradient",
    )(where, pieces, weight, upstream, following)


def latent_kernel(old_ref, act_ref, weight_ref, out_ref):
    total = jnp.dot(old_ref[...], weight_ref[0], preferred_element_type=F32)
    total = total + jnp.dot(act_ref[0], weight_ref[1], preferred_element_type=F32)
    total = total + jnp.dot(act_ref[1], weight_ref[2], preferred_element_type=F32)
    out_ref[...] = total.astype(BF16)


def temporal(oldest, acts, temporal_weight):
    positions, channels = oldest.shape
    out_channels = temporal_weight.shape[2]
    step = 512
    return pl.pallas_call(
        latent_kernel,
        grid=(positions // step,),
        in_specs=[
            pl.BlockSpec((step, channels), lambda i: (i, 0)),
            pl.BlockSpec((2, step, channels), lambda i: (0, i, 0)),
            pl.BlockSpec(temporal_weight.shape, lambda i: (0, 0, 0)),
        ],
        out_specs=pl.BlockSpec((step, out_channels), lambda i: (i, 0)),
        out_shape=jax.ShapeDtypeStruct((positions, out_channels), BF16),
        compiler_params=pltpu.CompilerParams(vmem_limit_bytes=VMEM_BYTES),
        cost_estimate=pl.CostEstimate(
            flops=6 * positions * channels * out_channels,
            bytes_accessed=6_000_000,
            transcendentals=0,
        ),
        name="temporal",
    )(oldest, acts, temporal_weight)


def total_kernel(parts_ref, after_ref, out_ref):
    total = jnp.sum(parts_ref[...].astype(F32), axis=0).astype(BF16)
    out_ref[...] = jnp.broadcast_to(total[None], out_ref.shape)


def total_for_all(parts, after):
    vmem = pl.BlockSpec(memory_space=pltpu.VMEM)
    return pl.pallas_call(
        total_kernel,
        in_specs=[vmem, pl.BlockSpec(memory_space=pl.ANY)],
        out_specs=vmem,
        out_shape=jax.ShapeDtypeStruct(parts.shape, BF16),
        compiler_params=pltpu.CompilerParams(vmem_limit_bytes=VMEM_BYTES),
        name="total_for_all",
    )(parts, after)


def unpack_kernel(where_ref, own_ref, away_ref, out_ref):
    side = where_ref[0]
    blocks = out_ref.shape[2] // LANES
    for ref, half in ((own_ref, side), (away_ref, 1 - side)):
        for p in range(away_ref.shape[0]):
            g, b = divmod(p, blocks)
            out_ref[half, g * PIECE : (g + 1) * PIECE, b * LANES : (b + 1) * LANES] = ref[p].astype(F32)


def unpack(where, own, away, height, width):
    vmem = pl.BlockSpec(memory_space=pltpu.VMEM)
    return pl.pallas_call(
        unpack_kernel,
        in_specs=[pl.BlockSpec(memory_space=pltpu.SMEM), vmem, vmem],
        out_specs=vmem,
        out_shape=jax.ShapeDtypeStruct((2, height // 2, width), F32),
        compiler_params=pltpu.CompilerParams(vmem_limit_bytes=VMEM_BYTES),
        name="unpack",
    )(where, own, away)


def body(video, spatial_weight, temporal_weight, latent_grad):
    tiles, chans = lax.axis_size("tile"), lax.axis_size("chan")
    devices = tiles * chans
    where = jnp.stack([lax.axis_index("segment"), lax.axis_index("tile")]).astype(jnp.int32)
    out_channels = latent_grad.shape[4]
    upstream = other_core(latent_grad)
    shift = [
        (s * tiles + j, (1 - s) * tiles + j - 1) for s in range(2) for j in range(1, tiles)
    ]
    following = lax.ppermute(latent_grad, ("segment", "tile"), shift)
    pieces = exchange(pack(video[0, :, 0], tiles, chans))
    acts, mine, sent = conv_and_gradient(
        where,
        pieces,
        spatial_weight,
        upstream.reshape((-1, out_channels)),
        following.reshape((-1, out_channels)),
    )
    oldest = lax.ppermute(acts[1], "tile", [(i, i + 1) for i in range(tiles - 1)])
    pair = (mine + other_core(sent)).astype(BF16)
    count = pair.shape[0]
    pair = jnp.pad(pair, ((0, devices - count), (0, 0), (0, 0)))
    whole = exchange(total_for_all(exchange(pair), oldest))[:count]
    grad = unpack(where, whole, other_core(whole), temporal_weight.shape[0] * temporal_weight.shape[1], out_channels)
    latents = temporal(oldest, acts, temporal_weight).reshape(upstream.shape)
    return (latents, grad.reshape(temporal_weight.shape))


def solution(mesh):
    placed = (
        P("segment", None, ("tile", "chan"), None, None),
        P(),
        P(),
        P("segment", "tile", None, "chan", None),
    )
    return jax.shard_map(
        body,
        mesh=mesh,
        in_specs=placed,
        out_specs=(P("segment", "tile", None, "chan", None), P()),
        check_vma=False,
    )
```

time: 232 us -> 184 us (0.79)
  matrix products: 27.8 us -> 0 us
  Pallas kernels: 0 us -> 20.5 us
  blocking collectives: 40.8 us -> 27.5 us
  local copies, waits for them, and re-layouts: 17.8 us -> 6.18 us
  starting transfers between devices: 48.7 us -> 41.5 us
  other arithmetic: 7.06 us -> 0.18 us
    ppermute x1 -> x2, waiting for transfers between devices: 8.32 us -> 80.4 us  [the longest x1 70.1 us: body(): following = lax.ppermute(latent_grad, ('segment', 'tile'), shift)]
    all_to_all x3 -> x2, waiting for transfers between devices: 78.3 us -> 6.52 us  [exchange(): lax.all_to_all(pieces, GROUP, split_axis=0, concat_axis=0, tiled=True)]
    pallas_call x0 -> x5, Pallas kernels: none -> 20.5 us  [the longest x1 10.6 us: conv_and_gradient(): pl.pallas_call(functools.partial(conv_kernel, rows, 32), in_specs=[pl.Blo...]
    dot_general x6 -> x0, matrix products: 19.6 us -> none  [the longest x3 11.9 us: body(): jnp.dot(tap, temporal_weight[k], preferred_element_type=jnp.float32)]
    all_to_all x1, blocking collectives: 40.8 us -> 27.5 us  [exchange(): lax.all_to_all(pieces, GROUP, split_axis=0, concat_axis=0, tiled=True)]
    conv_general_dilated x2 -> x0, matrix products: 8.24 us -> none  [activate(): lax.conv_general_dilated(columns[None], spatial_weight.reshape((3, 3, cha...]
    all_to_all x3 -> x2, starting transfers between devices: 37.3 us -> 31.5 us  [exchange(): lax.all_to_all(pieces, GROUP, split_axis=0, concat_axis=0, tiled=True)]
    concatenate x2 -> x0, other arithmetic: 4.92 us -> none  [the longest x1 3.61 us: column_windows(): return jnp.concatenate([left, blocks, right], axis=2)]
  transfers between devices with their start and end apart: 7 -> 7, of which waited for: 5 -> 3; matrix products, arithmetic and copies ran while one was open for 15% -> 1% of each run, Pallas kernels for 0% -> 2%
where the time goes in v2:
time: 184 us
  waiting for transfers between devices  86.9 us (47%)
  starting transfers between devices  41.5 us (23%)
  blocking collectives  27.5 us (15%)
  Pallas kernels  20.5 us (11%)
  local copies, waits for them, and re-layouts  6.18 us (3%)
    ppermute x1, waiting for transfers between devices, body(): following = lax.ppermute(latent_grad, ('segment', 'tile'), shift)  70.1 us
    all_to_all x2, starting transfers between devices, exchange(): lax.all_to_all(pieces, GROUP, split_axis=0, concat_axis=0, tiled=True)  31.5 us
    all_to_all x1, blocking collectives, exchange(): lax.all_to_all(pieces, GROUP, split_axis=0, concat_axis=0, tiled=True)  27.5 us
    pallas_call x1, Pallas kernels, conv_and_gradient(): pl.pallas_call(functools.partial(conv_kernel, rows, 32), in_specs=[pl.Blo...  10.6 us
    ppermute x1, waiting for transfers between devices, body(): lax.ppermute(acts[1], 'tile', [(i, i + 1) for i in range(tiles - 1)])  10.3 us
    all_to_all x2, waiting for transfers between devices, exchange(): lax.all_to_all(pieces, GROUP, split_axis=0, concat_axis=0, tiled=True)  6.52 us
    ppermute x3, starting transfers between devices, other_core(): return lax.ppermute(shard, 'segment', [(0, 1), (1, 0)])  5.04 us
    unnamed x8, local copies, waits for them, and re-layouts  4.27 us
  transfers between devices with their start and end apart: 7, of which 3 were waited for; matrix products, arithmetic and copies ran while one was open for 1% of the time, Pallas kernels for 2%

profile of v2, /device:TPU:1, one launch (start us, length us, event | category | flops | bytes accessed | tf_op | source)
XLA Modules:
  0.0 183.5 jit_solution(16921023036416906054)
XLA Ops:
  0.6 0.0 copy-start
  0.6 1.6 copy-done
  2.2 3.3 %pack.1 = bf16[128,72,128]{2,1,0:T(8,128)(2,1)} custom-call(bf16[16,256,256]{2,1,0:T(8,128)(2,1)S(1)} %bitcast.10, bf16[16,256,256]{2,1,0:T(8,128)(2,1)S(1)} %bitcast.11), custom_call_target="tpu_custom_call" | custom-call | tf_op jit(solution)/shard_map/pack/pallas_call | solution.py:50
  5.6 16.3 %all-to-all-start = ((bf16[128,72,128]{2,1,0:T(8,128)(2,1)}), bf16[128,72,128]{2,1,0:T(8,128)(2,1)S(1)}, u32[]{:S(2)}, u32[]{:S(2)}) async-start(bf16[128,72,128]{2,1,0:T(8,128)(2,1)} %pack.1), calls=%async_computation | async-start | bytes 4718592 | tf_op jit(solution)/shard_map/all_to_all | solution.py:20
  21.9 1.3 collective-permute-start.1
  23.2 1.0 collective-permute-start
  24.2 0.1 pad_add_fusion.where_ref
  24.3 70.1 %collective-permute-done.1 = bf16[1,1,128,16,512]{4,3,2,1,0:T(8,128)(2,1)} collective-permute-done((bf16[1,1,128,16,512]{4,3,2,1,0:T(8,128)(2,1)}, bf16[1,1,128,16,512]{4,3,2,1,0:T(8,128)(2,1)}, u32[]{:S(2)}, u32[]{:S(2)}) %collective-permute-start.1) | collective-permute-done | bytes 2097184 | tf_op jit(solution)/shard_map/ppermute | solution.py:244
  94.4 0.0 collective-permute-done
  94.4 0.0 all-to-all-done.y_hbm
  94.4 0.0 copy-start.3
  94.4 1.4 copy-done.3
  95.8 0.0 copy-start.2
  95.8 1.3 copy-done.2
  97.1 10.6 %conv_and_gradient.1 = (bf16[2,2048,256]{2,1,0:T(8,128)(2,1)S(1)}, f32[96,16,128]{2,1,0:T(8,128)S(1)}, f32[96,16,128]{2,1,0:T(8,128)S(1)}) custom-call(s32[2]{0:T(128)S(1)} %pad_add_fusion.where_ref, bf16[128,72,128]{2,1,0:T(8,128)(2,1)} %copy-done.3, bf16[3,768,256]{2,1,0:T(8,128)(2,1)S(1)} %bitcast.12, bf16[2048,512]{1,0:T(8,128)(2,1)} %bitcast.4.u_hbm, ...), custom_call_target="tpu_custom_call" | custom-call | flops 6442450944 | bytes 10000000 | tf_op jit(solution)/shard_map/conv_and_gradient/pallas_call | solution.py:142
  107.8 0.5 collective-permute-start.3
  108.2 1.0 slice_bitcast_fusion
  109.3 3.7 %collective-permute-start.2 = (bf16[2048,256]{1,0:T(8,128)(2,1)}, bf16[2048,256]{1,0:T(8,128)(2,1)S(1)}, u32[]{:S(2)}, u32[]{:S(2)}) collective-permute-start(bf16[2048,256]{1,0:T(8,128)(2,1)} %slice_bitcast_fusion), channel_id=1, source_target_pairs={{0,16},{16,32},{32,48},{48,64},{64,80},{80,96},{96,112},{1,17},{17... | collective-permute-start | bytes 3145736 | tf_op jit(solution)/shard_map/ppermute | solution.py:253
  113.0 0.0 collective-permute-done.3
  113.0 0.1 add_convert_fusion
  113.1 0.8 pad.4
  114.0 15.1 %all-to-all-start.1 = ((bf16[128,16,128]{2,1,0:T(8,128)(2,1)}), bf16[128,16,128]{2,1,0:T(8,128)(2,1)}, u32[]{:S(2)}, u32[]{:S(2)}) async-start(bf16[128,16,128]{2,1,0:T(8,128)(2,1)} %pad.4), calls=%async_computation.1 | async-start | bytes 1048576 | tf_op jit(solution)/shard_map/all_to_all | solution.py:20
  129.1 10.3 %collective-permute-done.2.old_ref.after_ref = bf16[2048,256]{1,0:T(8,128)(2,1)S(1)} collective-permute-done((bf16[2048,256]{1,0:T(8,128)(2,1)}, bf16[2048,256]{1,0:T(8,128)(2,1)S(1)}, u32[]{:S(2)}, u32[]{:S(2)}) %collective-permute-start.2) | collective-permute-done | bytes 1048608 | tf_op jit(solution)/shard_map/ppermute | solution.py:253
  139.4 6.5 %all-to-all-done.1.parts_ref = bf16[128,16,128]{2,1,0:T(8,128)(2,1)} async-done(((bf16[128,16,128]{2,1,0:T(8,128)(2,1)}), bf16[128,16,128]{2,1,0:T(8,128)(2,1)}, u32[]{:S(2)}, u32[]{:S(2)}) %all-to-all-start.1) | async-done | bytes 524320 | tf_op jit(solution)/shard_map/all_to_all | solution.py:20
  145.9 0.0 copy-start.1
  145.9 1.3 total_for_all.1
  147.2 27.5 %all_to_all.15 = bf16[128,16,128]{2,1,0:T(8,128)(2,1)S(1)} all-to-all(bf16[128,16,128]{2,1,0:T(8,128)(2,1)S(1)} %total_for_all.1), channel_id=1, replica_groups=mesh['segment'=2,'tile'=8,'chan'=16] {'tile','chan'}, dimensions={0} | all-to-all | bytes 1048576 | tf_op jit(solution)/shard_map/all_to_all | solution.py:20
  174.8 3.5 %collective-permute-start.4 = (bf16[96,16,128]{2,1,0:T(8,128)(2,1)S(1)}, bf16[96,16,128]{2,1,0:T(8,128)(2,1)S(1)}, u32[]{:S(2)}, u32[]{:S(2)}) collective-permute-start(bf16[96,16,128]{2,1,0:T(8,128)(2,1)S(1)} %slice.8.own_ref), channel_id=1, source_target_pairs={{0,128},{128,0},{1,129},{129,1},{2,130},{130,2},{3,131},{131,3},{4... | collective-permute-start | bytes 1179656 | tf_op jit(solution)/shard_map/ppermute | solution.py:24
  178.3 0.0 copy-done.1
  178.3 3.4 %temporal.1 = bf16[2048,512]{1,0:T(8,128)(2,1)} custom-call(bf16[2048,256]{1,0:T(8,128)(2,1)S(1)} %collective-permute-done.2.old_ref.after_ref, bf16[2,2048,256]{2,1,0:T(8,128)(2,1)S(1)} %get-tuple-element.5.act_ref, bf16[3,256,512]{2,1,0:T(8,128)(2,1)S(1)} %copy-done.1), custom_call_target="tpu_custom_call" | custom-call | flops 1610612736 | bytes 6000000 | tf_op jit(solution)/shard_map/temporal/pallas_call | solution.py:177
  181.7 0.0 collective-permute-done.4.away_ref
  181.7 1.8 unpack.1
  (1 shorter events, 0.0 us)
Async XLA Ops:
  0.6 1.6 copy-start
  5.6 88.9 %all-to-all-start = ((bf16[128,72,128]{2,1,0:T(8,128)(2,1)}), bf16[128,72,128]{2,1,0:T(8,128)(2,1)S(1)}, u32[]{:S(2)}, u32[]{:S(2)}) async-start(bf16[128,72,128]{2,1,0:T(8,128)(2,1)} %pack.1), calls=%async_computation | async-start | bytes 4718592 | tf_op jit(solution)/shard_map/all_to_all | solution.py:20
  21.9 72.5 %collective-permute-start.1 = (bf16[1,1,128,16,512]{4,3,2,1,0:T(8,128)(2,1)}, bf16[1,1,128,16,512]{4,3,2,1,0:T(8,128)(2,1)}, u32[]{:S(2)}, u32[]{:S(2)}) collective-permute-start(bf16[1,1,128,16,512]{4,3,2,1,0:T(8,128)(2,1)} %param.7), channel_id=1, source_target_pairs={{16,128},{32,144},{48,160},{64,176},{80,192},{96,208},{112,224},{1... | collective-permute-start | bytes 6291464 | tf_op jit(solution)/shard_map/ppermute | solution.py:244
  23.2 71.2 %collective-permute-start = (bf16[1,1,128,16,512]{4,3,2,1,0:T(8,128)(2,1)}, bf16[1,1,128,16,512]{4,3,2,1,0:T(8,128)(2,1)}, u32[]{:S(2)}, u32[]{:S(2)}) collective-permute-start(bf16[1,1,128,16,512]{4,3,2,1,0:T(8,128)(2,1)} %param.7), channel_id=1, source_target_pairs={{0,128},{128,0},{1,129},{129,1},{2,130},{130,2},{3,131},{131,3},{4... | collective-permute-start | bytes 6291464 | tf_op jit(solution)/shard_map/ppermute | solution.py:24
  94.4 1.4 copy-start.3
  95.8 1.3 copy-start.2
  107.8 5.3 %collective-permute-start.3 = (f32[96,16,128]{2,1,0:T(8,128)S(1)}, f32[96,16,128]{2,1,0:T(8,128)S(1)}, u32[]{:S(2)}, u32[]{:S(2)}) collective-permute-start(f32[96,16,128]{2,1,0:T(8,128)S(1)} %get-tuple-element.7), channel_id=1, source_target_pairs={{0,128},{128,0},{1,129},{129,1},{2,130},{130,2},{3,131},{131,3},{4... | collective-permute-start | bytes 2359304 | tf_op jit(solution)/shard_map/ppermute | solution.py:24
  109.3 30.1 %collective-permute-start.2 = (bf16[2048,256]{1,0:T(8,128)(2,1)}, bf16[2048,256]{1,0:T(8,128)(2,1)S(1)}, u32[]{:S(2)}, u32[]{:S(2)}) collective-permute-start(bf16[2048,256]{1,0:T(8,128)(2,1)} %slice_bitcast_fusion), channel_id=1, source_target_pairs={{0,16},{16,32},{32,48},{48,64},{64,80},{80,96},{96,112},{1,17},{17... | collective-permute-start | bytes 3145736 | tf_op jit(solution)/shard_map/ppermute | solution.py:253
  114.0 32.0 %all-to-all-start.1 = ((bf16[128,16,128]{2,1,0:T(8,128)(2,1)}), bf16[128,16,128]{2,1,0:T(8,128)(2,1)}, u32[]{:S(2)}, u32[]{:S(2)}) async-start(bf16[128,16,128]{2,1,0:T(8,128)(2,1)} %pad.4), calls=%async_computation.1 | async-start | bytes 1048576 | tf_op jit(solution)/shard_map/all_to_all | solution.py:20
  145.9 32.3 %copy-start.1 = (bf16[3,256,512]{2,1,0:T(8,128)(2,1)S(1)}, bf16[3,256,512]{2,1,0:T(8,128)(2,1)}, u32[]{:S(2)}) copy-start(bf16[3,256,512]{2,1,0:T(8,128)(2,1)} %weight_ref.1) | copy-start | bytes 2359300
  174.8 7.0 %collective-permute-start.4 = (bf16[96,16,128]{2,1,0:T(8,128)(2,1)S(1)}, bf16[96,16,128]{2,1,0:T(8,128)(2,1)S(1)}, u32[]{:S(2)}, u32[]{:S(2)}) collective-permute-start(bf16[96,16,128]{2,1,0:T(8,128)(2,1)S(1)} %slice.8.own_ref), channel_id=1, source_target_pairs={{0,128},{128,0},{1,129},{129,1},{2,130},{130,2},{3,131},{131,3},{4... | collective-permute-start | bytes 1179656 | tf_op jit(solution)/shard_map/ppermute | solution.py:24

commit v3 on v2

--- a/solution.py
+++ b/solution.py
@@ -11,7 +11,7 @@
 LANES = 128
 COLS = 16
 PIECE = 16
-VMEM_BYTES = 48 * 1024 * 1024
+VMEM_BYTES = 32 * 1024 * 1024
 F32 = jnp.float32
 BF16 = jnp.bfloat16
 
@@ -66,24 +66,24 @@
 
 
 def conv_kernel(
-    rows, chunk, where_ref, y_hbm, w_hbm, u_hbm, next_hbm,
-    act_ref, mine_ref, sent_ref, y_ref, w_ref, u_ref, next_ref, window_ref, grad_ref, sems,
+    rows, chunk, where_ref, y_hbm, w_hbm, odd_ref, even_ref, y_ref, w_ref, window_ref, y_sems, w_sem
 ):
-    copies = [
-        pltpu.make_async_copy(src, dst, sems.at[i])
-        for i, (src, dst) in enumerate(
-            ((y_hbm, y_ref), (w_hbm, w_ref), (u_hbm, u_ref), (next_hbm, next_ref))
-        )
-    ]
-    for copy in copies:
-        copy.start()
     channels = 2 * LANES
-    side, tile = where_ref[0], where_ref[1]
+    loads = []
+    for i, r in enumerate(range(0, rows, chunk)):
+        part = pl.ds(r, chunk)
+        loads.append(pltpu.make_async_copy(y_hbm.at[part], y_ref.at[part], y_sems.at[i]))
+    weights = pltpu.make_async_copy(w_hbm, w_ref, w_sem)
+    for load in loads:
+        load.start()
+    weights.start()
+    tile = where_ref[1]
     window_ref[0] = jnp.zeros(window_ref.shape[1:], BF16)
     window_ref[rows + 1] = jnp.zeros(window_ref.shape[1:], BF16)
-    copies[0].wait()
-    for f in (1, 0):
+    for f, act_ref in ((1, even_ref), (0, odd_ref)):
         for r in range(0, rows, chunk):
+            if f == 1:
+                loads[r // chunk].wait()
             place = lax.broadcasted_iota(jnp.int32, (chunk, COLS, LANES), 1)
             edges = y_ref[r : r + chunk, 4 * COLS :, :].astype(F32)
             for h in range(2):
@@ -100,7 +100,7 @@
                     lane = e * channels + h * LANES
                     window_ref[r + 1 : r + 1 + chunk, :, lane : lane + LANES] = part
         if f == 1:
-            copies[1].wait()
+            weights.wait()
         for r in range(0, rows, chunk):
             pre = jnp.zeros((chunk * COLS, channels), F32)
             for a in range(3):
@@ -109,14 +109,58 @@
             value = silu(pre)
             if f == 0:
                 value = jnp.where(tile > 0, value, jnp.zeros_like(value))
-            act_ref[f, r * COLS : (r + chunk) * COLS, :] = value.astype(BF16)
-    copies[2].wait()
-    copies[3].wait()
-    lanes = grad_ref.shape[1]
+            act_ref[r * COLS : (r + chunk) * COLS, :] = value.astype(BF16)
+
+
+def spatial(where, pieces, spatial_weight):
+    rows = pieces.shape[0]
+    channels = spatial_weight.shape[2]
+    positions = rows * COLS
+    chunk = 32
+    weight = spatial_weight.reshape((3, 3 * channels, channels))
+    hbm = pl.BlockSpec(memory_space=pltpu.HBM)
+    vmem = pl.BlockSpec(memory_space=pltpu.VMEM)
+    act = jax.ShapeDtypeStruct((positions, channels), BF16)
+    return pl.pallas_call(
+        functools.partial(conv_kernel, rows, chunk),
+        in_specs=[pl.BlockSpec(memory_space=pltpu.SMEM), hbm, hbm],
+        out_specs=[vmem, vmem],
+        out_shape=[act, act],
+        scratch_shapes=[
+            pltpu.VMEM(pieces.shape, BF16),
+            pltpu.VMEM(weight.shape, BF16),
+            pltpu.VMEM((rows + 2, COLS, 3 * channels), BF16),
+            pltpu.SemaphoreType.DMA((rows // chunk,)),
+            pltpu.SemaphoreType.DMA,
+        ],
+        compiler_params=pltpu.CompilerParams(vmem_limit_bytes=VMEM_BYTES),
+        cost_estimate=pl.CostEstimate(
+            flops=36 * positions * channels * channels,
+            bytes_accessed=6_000_000,
+            transcendentals=2 * positions * channels,
+        ),
+        name="spatial",
+    )(where, pieces, weight)
+
+
+def gradient_kernel(
+    where_ref, odd_ref, even_ref, u_hbm, next_hbm, mine_ref, sent_ref, u_ref, next_ref, grad_ref, sems
+):
+    loads = (
+        pltpu.make_async_copy(u_hbm, u_ref, sems.at[0]),
+        pltpu.make_async_copy(next_hbm, next_ref, sems.at[1]),
+    )
+    for load in loads:
+        load.start()
+    side = where_ref[0]
+    channels = odd_ref.shape[1]
     blocks = u_ref.shape[1] // LANES
-    for k, (f, up) in enumerate(((1, next_ref), (0, u_ref), (1, u_ref))):
+    loads[0].wait()
+    for k, act_ref, up in ((1, odd_ref, u_ref), (2, even_ref, u_ref), (0, even_ref, next_ref)):
+        if k == 0:
+            loads[1].wait()
         term = lax.dot_general(
-            act_ref[f], up[...], (((0,), (0,)), ((), ())), preferred_element_type=F32
+            act_ref[...], up[...], (((0,), (0,)), ((), ())), preferred_element_type=F32
         )
         for g in range(channels // PIECE):
             line = k * channels + g * PIECE
@@ -129,57 +173,53 @@
     sent_ref[...] = grad_ref[1 - side]
 
 
-def conv_and_gradient(where, pieces, spatial_weight, upstream, following):
-    rows = pieces.shape[0]
-    channels = spatial_weight.shape[2]
+def gradient(where, odd, even, upstream, following):
+    positions, channels = odd.shape
     out_channels = upstream.shape[1]
-    positions = rows * COLS
     count = 3 * channels * out_channels // (2 * PIECE * LANES)
-    hbm = pl.BlockSpec(memory_space=pl.ANY)
     vmem = pl.BlockSpec(memory_space=pltpu.VMEM)
-    weight = spatial_weight.reshape((3, 3 * channels, channels))
+    hbm = pl.BlockSpec(memory_space=pltpu.HBM)
     part = jax.ShapeDtypeStruct((count, PIECE, LANES), F32)
     return pl.pallas_call(
-        functools.partial(conv_kernel, rows, 32),
-        in_specs=[pl.BlockSpec(memory_space=pltpu.SMEM), hbm, hbm, hbm, hbm],
-        out_specs=[vmem, vmem, vmem],
-        out_shape=[jax.ShapeDtypeStruct((2, positions, channels), BF16), part, part],
+        gradient_kernel,
+        in_specs=[pl.BlockSpec(memory_space=pltpu.SMEM), vmem, vmem, hbm, hbm],
+        out_specs=[vmem, vmem],
+        out_shape=[part, part],
         scratch_shapes=[
-            pltpu.VMEM(pieces.shape, BF16),
-            pltpu.VMEM(weight.shape, BF16),
             pltpu.VMEM(upstream.shape, BF16),
             pltpu.VMEM(following.shape, BF16),
-            pltpu.VMEM((rows + 2, COLS, 3 * channels), BF16),
             pltpu.VMEM((2, count, PIECE, LANES), F32),
-            pltpu.SemaphoreType.DMA((4,)),
+            pltpu.SemaphoreType.DMA((2,)),
         ],
         compiler_params=pltpu.CompilerParams(vmem_limit_bytes=VMEM_BYTES),
         cost_estimate=pl.CostEstimate(
-            flops=2 * positions * (18 * channels * channels + 3 * channels * out_channels),
-            bytes_accessed=10_000_000,
-            transcendentals=2 * positions * channels,
+            flops=6 * positions * channels * out_channels,
+            bytes_accessed=8_000_000,
+            transcendentals=0,
         ),
-        name="conv_and_gradient",
-    )(where, pieces, weight, upstream, following)
-
-
-def latent_kernel(old_ref, act_ref, weight_ref, out_ref):
+        name="gradient",
+    )(where, odd, even, upstream, following)
+
+
+def latent_kernel(old_ref, odd_ref, even_ref, weight_ref, out_ref):
     total = jnp.dot(old_ref[...], weight_ref[0], preferred_element_type=F32)
-    total = total + jnp.dot(act_ref[0], weight_ref[1], preferred_element_type=F32)
-    total = total + jnp.dot(act_ref[1], weight_ref[2], preferred_element_type=F32)
+    total = total + jnp.dot(odd_ref[...], weight_ref[1], preferred_element_type=F32)
+    total = total + jnp.dot(even_ref[...], weight_ref[2], preferred_element_type=F32)
     out_ref[...] = total.astype(BF16)
 
 
-def temporal(oldest, acts, temporal_weight):
+def temporal(oldest, odd, even, temporal_weight):
     positions, channels = oldest.shape
     out_channels = temporal_weight.shape[2]
     step = 512
+    tap = pl.BlockSpec((step, channels), lambda i: (i, 0))
     return pl.pallas_call(
         latent_kernel,
         grid=(positions // step,),
         in_specs=[
-            pl.BlockSpec((step, channels), lambda i: (i, 0)),
-            pl.BlockSpec((2, step, channels), lambda i: (0, i, 0)),
+            tap,
+            tap,
+            tap,
             pl.BlockSpec(temporal_weight.shape, lambda i: (0, 0, 0)),
         ],
         out_specs=pl.BlockSpec((step, out_channels), lambda i: (i, 0)),
@@ -191,24 +231,24 @@
             transcendentals=0,
         ),
         name="temporal",
-    )(oldest, acts, temporal_weight)
-
-
-def total_kernel(parts_ref, after_ref, out_ref):
+    )(oldest, odd, even, temporal_weight)
+
+
+def total_kernel(parts_ref, out_ref):
     total = jnp.sum(parts_ref[...].astype(F32), axis=0).astype(BF16)
     out_ref[...] = jnp.broadcast_to(total[None], out_ref.shape)
 
 
-def total_for_all(parts, after):
+def total_for_all(parts):
     vmem = pl.BlockSpec(memory_space=pltpu.VMEM)
     return pl.pallas_call(
         total_kernel,
-        in_specs=[vmem, pl.BlockSpec(memory_space=pl.ANY)],
+        in_specs=[vmem],
         out_specs=vmem,
         out_shape=jax.ShapeDtypeStruct(parts.shape, BF16),
         compiler_params=pltpu.CompilerParams(vmem_limit_bytes=VMEM_BYTES),
         name="total_for_all",
-    )(parts, after)
+    )(parts)
 
 
 def unpack_kernel(where_ref, own_ref, away_ref, out_ref):
@@ -242,21 +282,26 @@
         (s * tiles + j, (1 - s) * tiles + j - 1) for s in range(2) for j in range(1, tiles)
     ]
     following = lax.ppermute(latent_grad, ("segment", "tile"), shift)
-    pieces = exchange(pack(video[0, :, 0], tiles, chans))
-    acts, mine, sent = conv_and_gradient(
+    frames = pltpu.with_memory_space_constraint(video[0, :, 0], pltpu.HBM)
+    pieces = pltpu.with_memory_space_constraint(exchange(pack(frames, tiles, chans)), pltpu.HBM)
+    odd, even = spatial(where, pieces, spatial_weight)
+    mine, sent = gradient(
         where,
-        pieces,
-        spatial_weight,
+        odd,
+        even,
         upstream.reshape((-1, out_channels)),
         following.reshape((-1, out_channels)),
     )
-    oldest = lax.ppermute(acts[1], "tile", [(i, i + 1) for i in range(tiles - 1)])
+    oldest = lax.ppermute(even, "tile", [(i, i + 1) for i in range(tiles - 1)])
     pair = (mine + other_core(sent)).astype(BF16)
     count = pair.shape[0]
     pair = jnp.pad(pair, ((0, devices - count), (0, 0), (0, 0)))
-    whole = exchange(total_for_all(exchange(pair), oldest))[:count]
-    grad = unpack(where, whole, other_core(whole), temporal_weight.shape[0] * temporal_weight.shape[1], out_channels)
-    latents = temporal(oldest, acts, temporal_weight).reshape(upstream.shape)
+    whole = exchange(total_for_all(exchange(pair)))
+    latents = temporal(oldest, odd, even, temporal_weight).reshape(upstream.shape)
+    whole, latents = lax.optimization_barrier((whole, latents))
+    whole = whole[:count]
+    height = temporal_weight.shape[0] * temporal_weight.shape[1]
+    grad = unpack(where, whole, other_core(whole), height, out_channels)
     return (latents, grad.reshape(temporal_weight.shape))
 
 

time: 184 us -> 168 us (0.913)
  blocking collectives: 27.5 us -> 0 us
  starting transfers between devices: 41.5 us -> 51.1 us
  Pallas kernels: 20.5 us -> 25.9 us
  local copies, waits for them, and re-layouts: 6.18 us -> 0.87 us
    all_to_all x2 -> x3, waiting for transfers between devices: 6.52 us -> 73.3 us  [exchange(): lax.all_to_all(pieces, GROUP, split_axis=0, concat_axis=0, tiled=True)]
    ppermute x1, waiting for transfers between devices: 70.1 us -> 9.52 us  [body(): following = lax.ppermute(latent_grad, ('segment', 'tile'), shift)]
    all_to_all x1 -> x0, blocking collectives: 27.5 us -> none  [exchange(): lax.all_to_all(pieces, GROUP, split_axis=0, concat_axis=0, tiled=True)]
    all_to_all x2 -> x3, starting transfers between devices: 31.5 us -> 41.6 us  [exchange(): lax.all_to_all(pieces, GROUP, split_axis=0, concat_axis=0, tiled=True)]
    ppermute x1, waiting for transfers between devices: 10.3 us -> 2.58 us  [body(): oldest = lax.ppermute(even, 'tile', [(i, i + 1) for i in range(tiles - 1)])]
    unnamed x8 -> x4, local copies, waits for them, and re-layouts: 4.27 us -> 0.01 us
    ppermute x3, waiting for transfers between devices: 0.01 us -> 3.26 us  [other_core(): return lax.ppermute(shard, 'segment', [(0, 1), (1, 0)])]
    pallas_call x1, Pallas kernels: 3.34 us -> 6.11 us  [pack(): pl.pallas_call(pack_kernel, grid=(tiles,), in_specs=[pl.BlockSpec((1, wid...]
  transfers between devices with their start and end apart: 7 -> 8, of which waited for: 3 -> 7; matrix products, arithmetic and copies ran while one was open for 1% -> 0% of each run, Pallas kernels for 2% -> 8%
where the time goes in v3:
time: 168 us
  waiting for transfers between devices  88.7 us (53%)
  starting transfers between devices  51.1 us (30%)
  Pallas kernels  25.9 us (15%)
    all_to_all x3, waiting for transfers between devices, exchange(): lax.all_to_all(pieces, GROUP, split_axis=0, concat_axis=0, tiled=True)  73.3 us
    all_to_all x3, starting transfers between devices, exchange(): lax.all_to_all(pieces, GROUP, split_axis=0, concat_axis=0, tiled=True)  41.6 us
    ppermute x1, waiting for transfers between devices, body(): following = lax.ppermute(latent_grad, ('segment', 'tile'), shift)  9.52 us
    pallas_call x1, Pallas kernels, spatial(): pl.pallas_call(functools.partial(conv_kernel, rows, chunk), in_specs=[pl....  8.17 us
    pallas_call x1, Pallas kernels, pack(): pl.pallas_call(pack_kernel, grid=(tiles,), in_specs=[pl.BlockSpec((1, wid...  6.11 us
    ppermute x3, starting transfers between devices, other_core(): return lax.ppermute(shard, 'segment', [(0, 1), (1, 0)])  4.81 us
    pallas_call x1, Pallas kernels, temporal(): pl.pallas_call(latent_kernel, grid=(positions // step,), in_specs=[tap, t...  4.65 us
    pallas_call x1, Pallas kernels, gradient(): pl.pallas_call(gradient_kernel, in_specs=[pl.BlockSpec(memory_space=pltpu...  4.26 us
  transfers between devices with their start and end apart: 8, of which 7 were waited for; matrix products, arithmetic and copies ran while one was open for 0% of the time, Pallas kernels for 8%

profile of v3, /device:TPU:1, one launch (start us, length us, event | category | flops | bytes accessed | tf_op | source)
XLA Modules:
  0.0 167.5 jit_solution(10555480877551543439)
XLA Ops:
  0.6 6.1 %pack.1 = bf16[128,72,128]{2,1,0:T(8,128)(2,1)} custom-call(bf16[16,256,256]{2,1,0:T(8,128)(2,1)} %bitcast.9, bf16[16,256,256]{2,1,0:T(8,128)(2,1)} %bitcast.10), custom_call_target="tpu_custom_call" | custom-call | tf_op jit(solution)/shard_map/pack/pallas_call | solution.py:50
  6.7 0.0 copy-start.1
  6.7 16.9 %all-to-all-start = ((bf16[128,72,128]{2,1,0:T(8,128)(2,1)}), bf16[128,72,128]{2,1,0:T(8,128)(2,1)}, u32[]{:S(2)}, u32[]{:S(2)}) async-start(bf16[128,72,128]{2,1,0:T(8,128)(2,1)} %pack.1), calls=%async_computation | async-start | bytes 4718592 | tf_op jit(solution)/shard_map/all_to_all | solution.py:20
  23.7 1.0 collective-permute-start
  24.7 1.3 collective-permute-start.1
  26.0 0.1 pad_add_fusion.where_ref
  26.1 51.9 %all-to-all-done.y_hbm = bf16[128,72,128]{2,1,0:T(8,128)(2,1)} async-done(((bf16[128,72,128]{2,1,0:T(8,128)(2,1)}), bf16[128,72,128]{2,1,0:T(8,128)(2,1)}, u32[]{:S(2)}, u32[]{:S(2)}) %all-to-all-start) | async-done | bytes 2359328 | tf_op jit(solution)/shard_map/all_to_all | solution.py:20
  78.0 0.0 copy-done.1
  78.0 8.2 %spatial.1 = (bf16[2048,256]{1,0:T(8,128)(2,1)S(1)}, bf16[2048,256]{1,0:T(8,128)(2,1)S(1)}) custom-call(s32[2]{0:T(128)S(1)} %pad_add_fusion.where_ref, bf16[128,72,128]{2,1,0:T(8,128)(2,1)} %all-to-all-done.y_hbm, bf16[3,768,256]{2,1,0:T(8,128)(2,1)S(1)} %bitcast.8), custom_call_target="tpu_custom_call" | custom-call | flops 4831838208 | bytes 6000000 | tf_op jit(solution)/shard_map/spatial/pallas_call | solution.py:124
  86.2 0.0 collective-permute-done
  86.2 9.5 %collective-permute-done.1 = bf16[1,1,128,16,512]{4,3,2,1,0:T(8,128)(2,1)} collective-permute-done((bf16[1,1,128,16,512]{4,3,2,1,0:T(8,128)(2,1)}, bf16[1,1,128,16,512]{4,3,2,1,0:T(8,128)(2,1)}, u32[]{:S(2)}, u32[]{:S(2)}) %collective-permute-start.1) | collective-permute-done | bytes 2097184 | tf_op jit(solution)/shard_map/ppermute | solution.py:284
  95.7 4.3 %gradient.1 = (f32[96,16,128]{2,1,0:T(8,128)S(1)}, f32[96,16,128]{2,1,0:T(8,128)S(1)}) custom-call(s32[2]{0:T(128)S(1)} %pad_add_fusion.where_ref, bf16[2048,256]{1,0:T(8,128)(2,1)S(1)} %get-tuple-element.8.odd_ref, bf16[2048,256]{1,0:T(8,128)(2,1)S(1)} %get-tuple-element.9.even_ref, bf16[2048,512]{1,0:T(8,128)(2,1)} %bitcast.4.u_hbm, ...), custom_call_target="tpu_custom_call" | custom-call | flops 1610612736 | bytes 8000000 | tf_op jit(solution)/shard_map/gradient/pallas_call | solution.py:183
  100.0 0.5 collective-permute-start.2
  100.5 1.9 %collective-permute-done.2 = f32[96,16,128]{2,1,0:T(8,128)S(1)} collective-permute-done((f32[96,16,128]{2,1,0:T(8,128)S(1)}, f32[96,16,128]{2,1,0:T(8,128)S(1)}, u32[]{:S(2)}, u32[]{:S(2)}) %collective-permute-start.2) | collective-permute-done | bytes 786464 | tf_op jit(solution)/shard_map/ppermute | solution.py:24
  102.4 0.1 add_convert_fusion
  102.5 0.0 copy-start
  102.5 0.8 pad.4
  103.4 15.0 %all-to-all-start.1 = ((bf16[128,16,128]{2,1,0:T(8,128)(2,1)}), bf16[128,16,128]{2,1,0:T(8,128)(2,1)S(1)}, u32[]{:S(2)}, u32[]{:S(2)}) async-start(bf16[128,16,128]{2,1,0:T(8,128)(2,1)} %pad.4), calls=%async_computation.1 | async-start | bytes 1048576 | tf_op jit(solution)/shard_map/all_to_all | solution.py:20
  118.4 3.5 %collective-permute-start.3 = (bf16[2048,256]{1,0:T(8,128)(2,1)S(1)}, bf16[2048,256]{1,0:T(8,128)(2,1)}, u32[]{:S(2)}, u32[]{:S(2)}) collective-permute-start(bf16[2048,256]{1,0:T(8,128)(2,1)S(1)} %get-tuple-element.9.even_ref), channel_id=1, source_target_pairs={{0,16},{16,32},{32,48},{48,64},{64,80},{80,96},{96,112},{1,17},{17... | collective-permute-start | bytes 3145736 | tf_op jit(solution)/shard_map/ppermute | solution.py:295
  121.9 13.0 %all-to-all-done.1.parts_ref = bf16[128,16,128]{2,1,0:T(8,128)(2,1)S(1)} async-done(((bf16[128,16,128]{2,1,0:T(8,128)(2,1)}), bf16[128,16,128]{2,1,0:T(8,128)(2,1)S(1)}, u32[]{:S(2)}, u32[]{:S(2)}) %all-to-all-start.1) | async-done | bytes 524320 | tf_op jit(solution)/shard_map/all_to_all | solution.py:20
  134.9 1.0 total_for_all.1
  135.9 9.6 %all-to-all-start.2 = ((bf16[128,16,128]{2,1,0:T(8,128)(2,1)}), bf16[128,16,128]{2,1,0:T(8,128)(2,1)S(1)}, u32[]{:S(2)}, u32[]{:S(2)}) async-start(bf16[128,16,128]{2,1,0:T(8,128)(2,1)} %total_for_all.1), calls=%async_computation.2 | async-start | bytes 1048576 | tf_op jit(solution)/shard_map/all_to_all | solution.py:20
  145.5 2.6 %collective-permute-done.3.old_ref = bf16[2048,256]{1,0:T(8,128)(2,1)} collective-permute-done((bf16[2048,256]{1,0:T(8,128)(2,1)S(1)}, bf16[2048,256]{1,0:T(8,128)(2,1)}, u32[]{:S(2)}, u32[]{:S(2)}) %collective-permute-start.3) | collective-permute-done | bytes 1048608 | tf_op jit(solution)/shard_map/ppermute | solution.py:295
  148.1 0.0 copy-done
  148.1 4.7 %temporal.1 = bf16[2048,512]{1,0:T(8,128)(2,1)} custom-call(bf16[2048,256]{1,0:T(8,128)(2,1)} %collective-permute-done.3.old_ref, bf16[2048,256]{1,0:T(8,128)(2,1)S(1)} %get-tuple-element.8.odd_ref, bf16[2048,256]{1,0:T(8,128)(2,1)S(1)} %get-tuple-element.9.even_ref, bf16[3,256,512]{2,1,0:T(8,128)(2,1)S(1)} %copy-done), custom_call_target="tpu_custom_call" | custom-call | flops 1610612736 | bytes 6000000 | tf_op jit(solution)/shard_map/temporal/pallas_call | solution.py:216
  152.7 8.3 %all-to-all-done.2 = bf16[128,16,128]{2,1,0:T(8,128)(2,1)S(1)} async-done(((bf16[128,16,128]{2,1,0:T(8,128)(2,1)}), bf16[128,16,128]{2,1,0:T(8,128)(2,1)S(1)}, u32[]{:S(2)}, u32[]{:S(2)}) %all-to-all-start.2) | async-done | bytes 524320 | tf_op jit(solution)/shard_map/all_to_all | solution.py:20
  161.1 3.3 %collective-permute-start.4 = (bf16[96,16,128]{2,1,0:T(8,128)(2,1)S(1)}, bf16[96,16,128]{2,1,0:T(8,128)(2,1)S(1)}, u32[]{:S(2)}, u32[]{:S(2)}) collective-permute-start(bf16[96,16,128]{2,1,0:T(8,128)(2,1)S(1)} %slice.3.own_ref), channel_id=1, source_target_pairs={{0,128},{128,0},{1,129},{129,1},{2,130},{130,2},{3,131},{131,3},{4... | collective-permute-start | bytes 1179656 | tf_op jit(solution)/shard_map/ppermute | solution.py:24
  164.4 1.3 collective-permute-done.4.away_ref
  165.7 1.8 %unpack.1 = f32[2,384,512]{2,1,0:T(8,128)} custom-call(s32[2]{0:T(128)S(1)} %pad_add_fusion.where_ref, bf16[96,16,128]{2,1,0:T(8,128)(2,1)S(1)} %slice.3.own_ref, bf16[96,16,128]{2,1,0:T(8,128)(2,1)S(1)} %collective-permute-done.4.away_ref), custom_call_target="tpu_custom_call" | custom-call | tf_op jit(solution)/shard_map/unpack/pallas_call | solution.py:265
  (1 shorter events, 0.0 us)
Async XLA Ops:
  6.7 71.3 %copy-start.1 = (bf16[9,256,256]{2,1,0:T(8,128)(2,1)S(1)}, bf16[9,256,256]{2,1,0:T(8,128)(2,1)}, u32[]{:S(2)}) copy-start(bf16[9,256,256]{2,1,0:T(8,128)(2,1)} %param.5) | copy-start | bytes 3538948
  6.7 71.3 %all-to-all-start = ((bf16[128,72,128]{2,1,0:T(8,128)(2,1)}), bf16[128,72,128]{2,1,0:T(8,128)(2,1)}, u32[]{:S(2)}, u32[]{:S(2)}) async-start(bf16[128,72,128]{2,1,0:T(8,128)(2,1)} %pack.1), calls=%async_computation | async-start | bytes 4718592 | tf_op jit(solution)/shard_map/all_to_all | solution.py:20
  23.7 62.5 %collective-permute-start = (bf16[1,1,128,16,512]{4,3,2,1,0:T(8,128)(2,1)}, bf16[1,1,128,16,512]{4,3,2,1,0:T(8,128)(2,1)}, u32[]{:S(2)}, u32[]{:S(2)}) collective-permute-start(bf16[1,1,128,16,512]{4,3,2,1,0:T(8,128)(2,1)} %param.7), channel_id=1, source_target_pairs={{0,128},{128,0},{1,129},{129,1},{2,130},{130,2},{3,131},{131,3},{4... | collective-permute-start | bytes 6291464 | tf_op jit(solution)/shard_map/ppermute | solution.py:24
  24.7 71.0 %collective-permute-start.1 = (bf16[1,1,128,16,512]{4,3,2,1,0:T(8,128)(2,1)}, bf16[1,1,128,16,512]{4,3,2,1,0:T(8,128)(2,1)}, u32[]{:S(2)}, u32[]{:S(2)}) collective-permute-start(bf16[1,1,128,16,512]{4,3,2,1,0:T(8,128)(2,1)} %param.7), channel_id=1, source_target_pairs={{16,128},{32,144},{48,160},{64,176},{80,192},{96,208},{112,224},{1... | collective-permute-start | bytes 6291464 | tf_op jit(solution)/shard_map/ppermute | solution.py:284
  100.0 2.4 %collective-permute-start.2 = (f32[96,16,128]{2,1,0:T(8,128)S(1)}, f32[96,16,128]{2,1,0:T(8,128)S(1)}, u32[]{:S(2)}, u32[]{:S(2)}) collective-permute-start(f32[96,16,128]{2,1,0:T(8,128)S(1)} %get-tuple-element.11), channel_id=1, source_target_pairs={{0,128},{128,0},{1,129},{129,1},{2,130},{130,2},{3,131},{131,3},{4... | collective-permute-start | bytes 2359304 | tf_op jit(solution)/shard_map/ppermute | solution.py:24
  102.5 45.6 %copy-start = (bf16[3,256,512]{2,1,0:T(8,128)(2,1)S(1)}, bf16[3,256,512]{2,1,0:T(8,128)(2,1)}, u32[]{:S(2)}) copy-start(bf16[3,256,512]{2,1,0:T(8,128)(2,1)} %weight_ref.1) | copy-start | bytes 2359300
  103.4 31.6 %all-to-all-start.1 = ((bf16[128,16,128]{2,1,0:T(8,128)(2,1)}), bf16[128,16,128]{2,1,0:T(8,128)(2,1)S(1)}, u32[]{:S(2)}, u32[]{:S(2)}) async-start(bf16[128,16,128]{2,1,0:T(8,128)(2,1)} %pad.4), calls=%async_computation.1 | async-start | bytes 1048576 | tf_op jit(solution)/shard_map/all_to_all | solution.py:20
  118.4 29.7 %collective-permute-start.3 = (bf16[2048,256]{1,0:T(8,128)(2,1)S(1)}, bf16[2048,256]{1,0:T(8,128)(2,1)}, u32[]{:S(2)}, u32[]{:S(2)}) collective-permute-start(bf16[2048,256]{1,0:T(8,128)(2,1)S(1)} %get-tuple-element.9.even_ref), channel_id=1, source_target_pairs={{0,16},{16,32},{32,48},{48,64},{64,80},{80,96},{96,112},{1,17},{17... | collective-permute-start | bytes 3145736 | tf_op jit(solution)/shard_map/ppermute | solution.py:295
  135.9 25.2 %all-to-all-start.2 = ((bf16[128,16,128]{2,1,0:T(8,128)(2,1)}), bf16[128,16,128]{2,1,0:T(8,128)(2,1)S(1)}, u32[]{:S(2)}, u32[]{:S(2)}) async-start(bf16[128,16,128]{2,1,0:T(8,128)(2,1)} %total_for_all.1), calls=%async_computation.2 | async-start | bytes 1048576 | tf_op jit(solution)/shard_map/all_to_all | solution.py:20
  161.1 4.6 %collective-permute-start.4 = (bf16[96,16,128]{2,1,0:T(8,128)(2,1)S(1)}, bf16[96,16,128]{2,1,0:T(8,128)(2,1)S(1)}, u32[]{:S(2)}, u32[]{:S(2)}) collective-permute-start(bf16[96,16,128]{2,1,0:T(8,128)(2,1)S(1)} %slice.3.own_ref), channel_id=1, source_target_pairs={{0,128},{128,0},{1,129},{129,1},{2,130},{130,2},{3,131},{131,3},{4... | collective-permute-start | bytes 1179656 | tf_op jit(solution)/shard_map/ppermute | solution.py:24

commit v4 on v3

--- a/solution.py
+++ b/solution.py
@@ -24,41 +24,73 @@
     return lax.ppermute(shard, "segment", [(0, 1), (1, 0)])
 
 
-def pack_kernel(odd_ref, even_ref, out_ref):
-    frames = (odd_ref[0], even_ref[0])
-    blocks, height = out_ref.shape[0], out_ref.shape[1]
-    place = lax.broadcasted_iota(jnp.int32, (blocks, 8, LANES), 1)
-    edges = jnp.zeros((blocks, 8, LANES), F32)
-    for f, frame in enumerate(frames):
-        for h in range(2):
-            half = frame[:, h * LANES : (h + 1) * LANES].reshape((blocks, COLS, LANES))
-            start = h * 2 * COLS + f * COLS
-            out_ref[:, start : start + COLS, :] = half
-            wide = half.astype(F32)
-            blank = jnp.zeros((1, 1, LANES), F32)
-            left = jnp.concatenate([blank, wide[:-1, COLS - 1 :]], axis=0)
-            right = jnp.concatenate([wide[1:, :1], blank], axis=0)
-            row = h * 4 + f * 2
-            edges = jnp.where(place == row, left, edges)
-            edges = jnp.where(place == row + 1, right, edges)
-    out_ref[:, height - 8 :, :] = edges.astype(BF16)
+def pack_kernel(tiles, chans, frame_hbm, out_hbm, frame_ref, piece_ref, in_sems, out_sems):
+    num = frame_hbm.shape[0]
+    height = piece_ref.shape[1]
+    loads = {}
+    for j in range(tiles):
+        for f in ((2 * j - 1) % num, 2 * j):
+            loads[f] = pltpu.make_async_copy(frame_hbm.at[f], frame_ref.at[f], in_sems.at[f])
+            loads[f].start()
+    stores = []
+    place = lax.broadcasted_iota(jnp.int32, (chans, 8, LANES), 1)
+    blank = jnp.zeros((1, 1, LANES), F32)
+    for j in range(tiles):
+        edges = jnp.zeros((chans, 8, LANES), F32)
+        block = pl.ds(j * chans, chans)
+        for f, source in enumerate(((2 * j - 1) % num, 2 * j)):
+            loads[source].wait()
+            for h in range(2):
+                half = frame_ref[source, :, h * LANES : (h + 1) * LANES]
+                half = half.reshape((chans, COLS, LANES))
+                start = h * 2 * COLS + f * COLS
+                piece_ref[block, start : start + COLS, :] = half
+                wide = half.astype(F32)
+                left = jnp.concatenate([blank, wide[:-1, COLS - 1 :]], axis=0)
+                right = jnp.concatenate([wide[1:, :1], blank], axis=0)
+                row = h * 4 + f * 2
+                edges = jnp.where(place == row, left, edges)
+                edges = jnp.where(place == row + 1, right, edges)
+        piece_ref[block, height - 8 :, :] = edges.astype(BF16)
+        stores.append(pltpu.make_async_copy(piece_ref.at[block], out_hbm.at[block], out_sems.at[j]))
+        stores[-1].start()
+    for store in stores:
+        store.wait()
 
 
 def pack(frames, tiles, chans):
-    num, width, channels = frames.shape
-    height = 4 * COLS + 8
-    return pl.pallas_call(
-        pack_kernel,
-        grid=(tiles,),
-        in_specs=[
-            pl.BlockSpec((1, width, channels), lambda j: ((2 * j + num - 1) % num, 0, 0)),
-            pl.BlockSpec((1, width, channels), lambda j: (2 * j, 0, 0)),
+    hbm = pl.BlockSpec(memory_space=pltpu.HBM)
+    pieces = jax.ShapeDtypeStruct((tiles * chans, 4 * COLS + 8, LANES), BF16)
+    return pl.pallas_call(
+        functools.partial(pack_kernel, tiles, chans),
+        in_specs=[hbm],
+        out_specs=hbm,
+        out_shape=pieces,
+        scratch_shapes=[
+            pltpu.VMEM(frames.shape, BF16),
+            pltpu.VMEM(pieces.shape, BF16),
+            pltpu.SemaphoreType.DMA((frames.shape[0],)),
+            pltpu.SemaphoreType.DMA((tiles,)),
         ],
-        out_specs=pl.BlockSpec((chans, height, LANES), lambda j: (j, 0, 0)),
-        out_shape=jax.ShapeDtypeStruct((tiles * chans, height, LANES), BF16),
         compiler_params=pltpu.CompilerParams(vmem_limit_bytes=VMEM_BYTES),
         name="pack",
-    )(frames, frames)
+    )(frames)
+
+
+def mask_kernel(where_ref, out_ref):
+    tile = where_ref[1]
+    out_ref[...] = jnp.where(tile > 0, jnp.ones(out_ref.shape, F32), jnp.zeros(out_ref.shape, F32))
+
+
+def odd_mask(where, channels):
+    return pl.pallas_call(
+        mask_kernel,
+        in_specs=[pl.BlockSpec(memory_space=pltpu.SMEM)],
+        out_specs=pl.BlockSpec(memory_space=pltpu.VMEM),
+        out_shape=jax.ShapeDtypeStruct((8, channels), F32),
+        cost_estimate=pl.CostEstimate(flops=10**12, bytes_accessed=10**9, transcendentals=0),
+        name="odd_mask",
+    )(where)
 
 
 def silu(pre):
@@ -66,7 +98,8 @@
 
 
 def conv_kernel(
-    rows, chunk, where_ref, y_hbm, w_hbm, odd_ref, even_ref, y_ref, w_ref, window_ref, y_sems, w_sem
+    rows, chunk, mask_hbm, y_hbm, w_hbm, odd_ref, even_ref,
+    mask_ref, y_ref, w_ref, window_ref, y_sems, w_sem, mask_sem,
 ):
     channels = 2 * LANES
     loads = []
@@ -77,7 +110,8 @@
     for load in loads:
         load.start()
     weights.start()
-    tile = where_ref[1]
+    mask = pltpu.make_async_copy(mask_hbm, mask_ref, mask_sem)
+    mask.start()
     window_ref[0] = jnp.zeros(window_ref.shape[1:], BF16)
     window_ref[rows + 1] = jnp.zeros(window_ref.shape[1:], BF16)
     for f, act_ref in ((1, even_ref), (0, odd_ref)):
@@ -101,6 +135,8 @@
                     window_ref[r + 1 : r + 1 + chunk, :, lane : lane + LANES] = part
         if f == 1:
             weights.wait()
+            mask.wait()
+            keep = mask_ref[0:1, :] > 0
         for r in range(0, rows, chunk):
             pre = jnp.zeros((chunk * COLS, channels), F32)
             for a in range(3):
@@ -108,11 +144,11 @@
                 pre = pre + jnp.dot(lhs, w_ref[a], preferred_element_type=F32)
             value = silu(pre)
             if f == 0:
-                value = jnp.where(tile > 0, value, jnp.zeros_like(value))
+                value = jnp.where(keep, value, jnp.zeros_like(value))
             act_ref[r * COLS : (r + chunk) * COLS, :] = value.astype(BF16)
 
 
-def spatial(where, pieces, spatial_weight):
+def spatial(mask, pieces, spatial_weight):
     rows = pieces.shape[0]
     channels = spatial_weight.shape[2]
     positions = rows * COLS
@@ -123,14 +159,16 @@
     act = jax.ShapeDtypeStruct((positions, channels), BF16)
     return pl.pallas_call(
         functools.partial(conv_kernel, rows, chunk),
-        in_specs=[pl.BlockSpec(memory_space=pltpu.SMEM), hbm, hbm],
+        in_specs=[hbm, hbm, hbm],
         out_specs=[vmem, vmem],
         out_shape=[act, act],
         scratch_shapes=[
+            pltpu.VMEM(mask.shape, F32),
             pltpu.VMEM(pieces.shape, BF16),
             pltpu.VMEM(weight.shape, BF16),
             pltpu.VMEM((rows + 2, COLS, 3 * channels), BF16),
             pltpu.SemaphoreType.DMA((rows // chunk,)),
+            pltpu.SemaphoreType.DMA,
             pltpu.SemaphoreType.DMA,
         ],
         compiler_params=pltpu.CompilerParams(vmem_limit_bytes=VMEM_BYTES),
@@ -140,7 +178,7 @@
             transcendentals=2 * positions * channels,
         ),
         name="spatial",
-    )(where, pieces, weight)
+    )(mask, pieces, weight)
 
 
 def gradient_kernel(
@@ -234,6 +272,24 @@
     )(oldest, odd, even, temporal_weight)
 
 
+def pair_kernel(mine_ref, away_ref, out_ref):
+    count = mine_ref.shape[0]
+    out_ref[:count] = (mine_ref[...] + away_ref[...]).astype(BF16)
+    out_ref[count:] = jnp.zeros((out_ref.shape[0] - count, *out_ref.shape[1:]), BF16)
+
+
+def pair_sum(mine, away, devices):
+    vmem = pl.BlockSpec(memory_space=pltpu.VMEM)
+    return pl.pallas_call(
+        pair_kernel,
+        in_specs=[vmem, vmem],
+        out_specs=vmem,
+        out_shape=jax.ShapeDtypeStruct((devices, *mine.shape[1:]), BF16),
+        compiler_params=pltpu.CompilerParams(vmem_limit_bytes=VMEM_BYTES),
+        name="pair_sum",
+    )(mine, away)
+
+
 def total_kernel(parts_ref, out_ref):
     total = jnp.sum(parts_ref[...].astype(F32), axis=0).astype(BF16)
     out_ref[...] = jnp.broadcast_to(total[None], out_ref.shape)
@@ -255,7 +311,7 @@
     side = where_ref[0]
     blocks = out_ref.shape[2] // LANES
     for ref, half in ((own_ref, side), (away_ref, 1 - side)):
-        for p in range(away_ref.shape[0]):
+        for p in range(out_ref.shape[1] // PIECE * blocks):
             g, b = divmod(p, blocks)
             out_ref[half, g * PIECE : (g + 1) * PIECE, b * LANES : (b + 1) * LANES] = ref[p].astype(F32)
 
@@ -284,7 +340,8 @@
     following = lax.ppermute(latent_grad, ("segment", "tile"), shift)
     frames = pltpu.with_memory_space_constraint(video[0, :, 0], pltpu.HBM)
     pieces = pltpu.with_memory_space_constraint(exchange(pack(frames, tiles, chans)), pltpu.HBM)
-    odd, even = spatial(where, pieces, spatial_weight)
+    mask = pltpu.with_memory_space_constraint(odd_mask(where, video.shape[4]), pltpu.HBM)
+    odd, even = spatial(mask, pieces, spatial_weight)
     mine, sent = gradient(
         where,
         odd,
@@ -293,13 +350,10 @@
         following.reshape((-1, out_channels)),
     )
     oldest = lax.ppermute(even, "tile", [(i, i + 1) for i in range(tiles - 1)])
-    pair = (mine + other_core(sent)).astype(BF16)
-    count = pair.shape[0]
-    pair = jnp.pad(pair, ((0, devices - count), (0, 0), (0, 0)))
+    pair = pair_sum(mine, other_core(sent), devices)
     whole = exchange(total_for_all(exchange(pair)))
     latents = temporal(oldest, odd, even, temporal_weight).reshape(upstream.shape)
     whole, latents = lax.optimization_barrier((whole, latents))
-    whole = whole[:count]
     height = temporal_weight.shape[0] * temporal_weight.shape[1]
     grad = unpack(where, whole, other_core(whole), height, out_channels)
     return (latents, grad.reshape(temporal_weight.shape))

time: 168 us -> 165 us (0.982)
  waiting for transfers between devices: 88.7 us -> 82.3 us
  starting transfers between devices: 51.1 us -> 56.1 us
    ppermute x1, waiting for transfers between devices: 9.52 us -> 0.01 us  [body(): following = lax.ppermute(latent_grad, ('segment', 'tile'), shift)]
    ppermute x3, starting transfers between devices: 4.81 us -> 8.34 us  [other_core(): return lax.ppermute(shard, 'segment', [(0, 1), (1, 0)])]
    all_to_all x3, waiting for transfers between devices: 73.3 us -> 76.3 us  [exchange(): lax.all_to_all(pieces, GROUP, split_axis=0, concat_axis=0, tiled=True)]
    pallas_call x2 -> x4, Pallas kernels: 14.3 us -> 12.6 us  [the longest x1 7.64 us: spatial(): pl.pallas_call(functools.partial(conv_kernel, rows, chunk), in_specs=[hbm...]
  transfers between devices with their start and end apart: 8 -> 8, of which waited for: 7 -> 6; matrix products, arithmetic and copies ran while one was open for 0% -> 0% of each run, Pallas kernels for 8% -> 11%
where the time goes in v4:
time: 165 us; the launch traced here: 164 us
  waiting for transfers between devices  82.3 us (50%)
  starting transfers between devices  56.1 us (34%)
  Pallas kernels  24.3 us (15%)
    all_to_all x3, waiting for transfers between devices, exchange(): lax.all_to_all(pieces, GROUP, split_axis=0, concat_axis=0, tiled=True)  76.3 us
    all_to_all x3, starting transfers between devices, exchange(): lax.all_to_all(pieces, GROUP, split_axis=0, concat_axis=0, tiled=True)  43 us
    ppermute x3, starting transfers between devices, other_core(): return lax.ppermute(shard, 'segment', [(0, 1), (1, 0)])  8.34 us
    pallas_call x1, Pallas kernels, spatial(): pl.pallas_call(functools.partial(conv_kernel, rows, chunk), in_specs=[hbm...  7.64 us
    pallas_call x1, Pallas kernels, temporal(): pl.pallas_call(latent_kernel, grid=(positions // step,), in_specs=[tap, t...  4.65 us
    pallas_call x1, Pallas kernels, gradient(): pl.pallas_call(gradient_kernel, in_specs=[pl.BlockSpec(memory_space=pltpu...  4.27 us
    ppermute x1, starting transfers between devices, body(): oldest = lax.ppermute(even, 'tile', [(i, i + 1) for i in range(tiles - 1)])  3.47 us
    ppermute x3, waiting for transfers between devices, other_core(): return lax.ppermute(shard, 'segment', [(0, 1), (1, 0)])  3.45 us
  transfers between devices with their start and end apart: 8, of which 6 were waited for; matrix products, arithmetic and copies ran while one was open for 0% of the time, Pallas kernels for 11%

profile of v4, /device:TPU:1, one launch (start us, length us, event | category | flops | bytes accessed | tf_op | source)
XLA Modules:
  0.0 164.0 jit_solution(7405782887964613837)
XLA Ops:
  0.6 3.3 %collective-permute-start = (bf16[1,1,128,16,512]{4,3,2,1,0:T(8,128)(2,1)}, bf16[1,1,128,16,512]{4,3,2,1,0:T(8,128)(2,1)}, u32[]{:S(2)}, u32[]{:S(2)}) collective-permute-start(bf16[1,1,128,16,512]{4,3,2,1,0:T(8,128)(2,1)} %param.7), channel_id=1, source_target_pairs={{0,128},{128,0},{1,129},{129,1},{2,130},{130,2},{3,131},{131,3},{4... | collective-permute-start | bytes 6291464 | tf_op jit(solution)/shard_map/ppermute | solution.py:24
  4.0 1.3 collective-permute-start.1
  5.2 2.7 %pack.1 = bf16[128,72,128]{2,1,0:T(8,128)(2,1)} custom-call(bf16[16,256,256]{2,1,0:T(8,128)(2,1)} %bitcast.10), custom_call_target="tpu_custom_call" | custom-call | tf_op jit(solution)/shard_map/pack/pallas_call | solution.py:64
  7.9 16.2 %all-to-all-start = ((bf16[128,72,128]{2,1,0:T(8,128)(2,1)}), bf16[128,72,128]{2,1,0:T(8,128)(2,1)}, u32[]{:S(2)}, u32[]{:S(2)}) async-start(bf16[128,72,128]{2,1,0:T(8,128)(2,1)} %pack.1), calls=%async_computation | async-start | bytes 4718592 | tf_op jit(solution)/shard_map/all_to_all | solution.py:20
  24.1 0.6 pad_add_fusion.where_ref
  24.7 0.0 copy-start.2
  24.7 1.4 odd_mask.1.mask_hbm
  26.1 55.2 %all-to-all-done.y_hbm = bf16[128,72,128]{2,1,0:T(8,128)(2,1)} async-done(((bf16[128,72,128]{2,1,0:T(8,128)(2,1)}), bf16[128,72,128]{2,1,0:T(8,128)(2,1)}, u32[]{:S(2)}, u32[]{:S(2)}) %all-to-all-start) | async-done | bytes 2359328 | tf_op jit(solution)/shard_map/all_to_all | solution.py:20
  81.3 0.0 copy-done.2
  81.3 0.0 copy-start.1
  81.3 7.6 %spatial.1 = (bf16[2048,256]{1,0:T(8,128)(2,1)S(1)}, bf16[2048,256]{1,0:T(8,128)(2,1)S(1)}) custom-call(f32[8,256]{1,0:T(8,128)} %odd_mask.1.mask_hbm, bf16[128,72,128]{2,1,0:T(8,128)(2,1)} %all-to-all-done.y_hbm, bf16[3,768,256]{2,1,0:T(8,128)(2,1)S(1)} %bitcast.8), custom_call_target="tpu_custom_call" | custom-call | flops 4831838208 | bytes 6000000 | tf_op jit(solution)/shard_map/spatial/pallas_call | solution.py:160
  88.9 0.0 collective-permute-done
  89.0 0.0 collective-permute-done.1
  89.0 0.0 copy-done.1
  89.0 4.3 %gradient.1 = (f32[96,16,128]{2,1,0:T(8,128)S(1)}, f32[96,16,128]{2,1,0:T(8,128)S(1)}) custom-call(s32[2]{0:T(128)S(1)} %copy-done.1, bf16[2048,256]{1,0:T(8,128)(2,1)S(1)} %get-tuple-element.8.odd_ref, bf16[2048,256]{1,0:T(8,128)(2,1)S(1)} %get-tuple-element.9.even_ref, bf16[2048,512]{1,0:T(8,128)(2,1)} %bitcast.4.u_hbm, bf16[2048,512]{1,0:T(8,128)(2,1)} %bitcast.5.next_hbm), custom_call_target="tpu_custom_call" | custom-call | flops 1610612736 | bytes 8000000 | tf_op jit(solution)/shard_map/gradient/pallas_call | solution.py:221
  93.3 1.8 %collective-permute-start.2 = (f32[96,16,128]{2,1,0:T(8,128)S(1)}, f32[96,16,128]{2,1,0:T(8,128)S(1)}, u32[]{:S(2)}, u32[]{:S(2)}) collective-permute-start(f32[96,16,128]{2,1,0:T(8,128)S(1)} %get-tuple-element.11), channel_id=1, source_target_pairs={{0,128},{128,0},{1,129},{129,1},{2,130},{130,2},{3,131},{131,3},{4... | collective-permute-start | bytes 2359304 | tf_op jit(solution)/shard_map/ppermute | solution.py:24
  95.0 1.9 %collective-permute-done.2.away_ref = f32[96,16,128]{2,1,0:T(8,128)S(1)} collective-permute-done((f32[96,16,128]{2,1,0:T(8,128)S(1)}, f32[96,16,128]{2,1,0:T(8,128)S(1)}, u32[]{:S(2)}, u32[]{:S(2)}) %collective-permute-start.2) | collective-permute-done | bytes 786464 | tf_op jit(solution)/shard_map/ppermute | solution.py:24
  96.9 0.9 pair_sum.1
  97.8 0.0 copy-start
  97.8 17.0 %all-to-all-start.1 = ((bf16[128,16,128]{2,1,0:T(8,128)(2,1)}), bf16[128,16,128]{2,1,0:T(8,128)(2,1)S(1)}, u32[]{:S(2)}, u32[]{:S(2)}) async-start(bf16[128,16,128]{2,1,0:T(8,128)(2,1)} %pair_sum.1), calls=%async_computation.1 | async-start | bytes 1048576 | tf_op jit(solution)/shard_map/all_to_all | solution.py:20
  114.9 3.5 %collective-permute-start.3 = (bf16[2048,256]{1,0:T(8,128)(2,1)S(1)}, bf16[2048,256]{1,0:T(8,128)(2,1)}, u32[]{:S(2)}, u32[]{:S(2)}) collective-permute-start(bf16[2048,256]{1,0:T(8,128)(2,1)S(1)} %get-tuple-element.9.even_ref), channel_id=1, source_target_pairs={{0,16},{16,32},{32,48},{48,64},{64,80},{80,96},{96,112},{1,17},{17... | collective-permute-start | bytes 3145736 | tf_op jit(solution)/shard_map/ppermute | solution.py:352
  118.3 12.8 %all-to-all-done.1.parts_ref = bf16[128,16,128]{2,1,0:T(8,128)(2,1)S(1)} async-done(((bf16[128,16,128]{2,1,0:T(8,128)(2,1)}), bf16[128,16,128]{2,1,0:T(8,128)(2,1)S(1)}, u32[]{:S(2)}, u32[]{:S(2)}) %all-to-all-start.1) | async-done | bytes 524320 | tf_op jit(solution)/shard_map/all_to_all | solution.py:20
  131.2 1.0 total_for_all.1
  132.1 9.8 %all-to-all-start.2 = ((bf16[128,16,128]{2,1,0:T(8,128)(2,1)}), bf16[128,16,128]{2,1,0:T(8,128)(2,1)S(1)}, u32[]{:S(2)}, u32[]{:S(2)}) async-start(bf16[128,16,128]{2,1,0:T(8,128)(2,1)} %total_for_all.1), calls=%async_computation.2 | async-start | bytes 1048576 | tf_op jit(solution)/shard_map/all_to_all | solution.py:20
  141.9 2.5 %collective-permute-done.3.old_ref = bf16[2048,256]{1,0:T(8,128)(2,1)} collective-permute-done((bf16[2048,256]{1,0:T(8,128)(2,1)S(1)}, bf16[2048,256]{1,0:T(8,128)(2,1)}, u32[]{:S(2)}, u32[]{:S(2)}) %collective-permute-start.3) | collective-permute-done | bytes 1048608 | tf_op jit(solution)/shard_map/ppermute | solution.py:352
  144.5 0.0 copy-done
  144.5 4.6 %temporal.1 = bf16[2048,512]{1,0:T(8,128)(2,1)} custom-call(bf16[2048,256]{1,0:T(8,128)(2,1)} %collective-permute-done.3.old_ref, bf16[2048,256]{1,0:T(8,128)(2,1)S(1)} %get-tuple-element.8.odd_ref, bf16[2048,256]{1,0:T(8,128)(2,1)S(1)} %get-tuple-element.9.even_ref, bf16[3,256,512]{2,1,0:T(8,128)(2,1)S(1)} %copy-done), custom_call_target="tpu_custom_call" | custom-call | flops 1610612736 | bytes 6000000 | tf_op jit(solution)/shard_map/temporal/pallas_call | solution.py:254
  149.1 8.3 %all-to-all-done.2.own_ref = bf16[128,16,128]{2,1,0:T(8,128)(2,1)S(1)} async-done(((bf16[128,16,128]{2,1,0:T(8,128)(2,1)}), bf16[128,16,128]{2,1,0:T(8,128)(2,1)S(1)}, u32[]{:S(2)}, u32[]{:S(2)}) %all-to-all-start.2) | async-done | bytes 524320 | tf_op jit(solution)/shard_map/all_to_all | solution.py:20
  157.5 3.2 %collective-permute-start.4 = (bf16[128,16,128]{2,1,0:T(8,128)(2,1)S(1)}, bf16[128,16,128]{2,1,0:T(8,128)(2,1)S(1)}, u32[]{:S(2)}, u32[]{:S(2)}) collective-permute-start(bf16[128,16,128]{2,1,0:T(8,128)(2,1)S(1)} %all-to-all-done.2.own_ref), channel_id=1, source_target_pairs={{0,128},{128,0},{1,129},{129,1},{2,130},{130,2},{3,131},{131,3},{4... | collective-permute-start | bytes 1572872 | tf_op jit(solution)/shard_map/ppermute | solution.py:24
  160.7 1.5 collective-permute-done.4.away_ref
  162.2 1.8 %unpack.1 = f32[2,384,512]{2,1,0:T(8,128)} custom-call(s32[2]{0:T(128)S(1)} %copy-done.1, bf16[128,16,128]{2,1,0:T(8,128)(2,1)S(1)} %all-to-all-done.2.own_ref, bf16[128,16,128]{2,1,0:T(8,128)(2,1)S(1)} %collective-permute-done.4.away_ref), custom_call_target="tpu_custom_call" | custom-call | tf_op jit(solution)/shard_map/unpack/pallas_call | solution.py:321
Async XLA Ops:
  0.6 88.3 %collective-permute-start = (bf16[1,1,128,16,512]{4,3,2,1,0:T(8,128)(2,1)}, bf16[1,1,128,16,512]{4,3,2,1,0:T(8,128)(2,1)}, u32[]{:S(2)}, u32[]{:S(2)}) collective-permute-start(bf16[1,1,128,16,512]{4,3,2,1,0:T(8,128)(2,1)} %param.7), channel_id=1, source_target_pairs={{0,128},{128,0},{1,129},{129,1},{2,130},{130,2},{3,131},{131,3},{4... | collective-permute-start | bytes 6291464 | tf_op jit(solution)/shard_map/ppermute | solution.py:24
  4.0 85.0 %collective-permute-start.1 = (bf16[1,1,128,16,512]{4,3,2,1,0:T(8,128)(2,1)}, bf16[1,1,128,16,512]{4,3,2,1,0:T(8,128)(2,1)}, u32[]{:S(2)}, u32[]{:S(2)}) collective-permute-start(bf16[1,1,128,16,512]{4,3,2,1,0:T(8,128)(2,1)} %param.7), channel_id=1, source_target_pairs={{16,128},{32,144},{48,160},{64,176},{80,192},{96,208},{112,224},{1... | collective-permute-start | bytes 6291464 | tf_op jit(solution)/shard_map/ppermute | solution.py:340
  7.9 73.4 %all-to-all-start = ((bf16[128,72,128]{2,1,0:T(8,128)(2,1)}), bf16[128,72,128]{2,1,0:T(8,128)(2,1)}, u32[]{:S(2)}, u32[]{:S(2)}) async-start(bf16[128,72,128]{2,1,0:T(8,128)(2,1)} %pack.1), calls=%async_computation | async-start | bytes 4718592 | tf_op jit(solution)/shard_map/all_to_all | solution.py:20
  24.7 56.6 %copy-start.2 = (bf16[9,256,256]{2,1,0:T(8,128)(2,1)S(1)}, bf16[9,256,256]{2,1,0:T(8,128)(2,1)}, u32[]{:S(2)}) copy-start(bf16[9,256,256]{2,1,0:T(8,128)(2,1)} %param.5) | copy-start | bytes 3538948
  81.3 7.7 %copy-start.1 = (s32[2]{0:T(128)S(1)}, s32[2]{0:T(128)}, u32[]{:S(2)}) copy-start(s32[2]{0:T(128)} %pad_add_fusion.where_ref) | copy-start | bytes 28
  93.3 3.7 %collective-permute-start.2 = (f32[96,16,128]{2,1,0:T(8,128)S(1)}, f32[96,16,128]{2,1,0:T(8,128)S(1)}, u32[]{:S(2)}, u32[]{:S(2)}) collective-permute-start(f32[96,16,128]{2,1,0:T(8,128)S(1)} %get-tuple-element.11), channel_id=1, source_target_pairs={{0,128},{128,0},{1,129},{129,1},{2,130},{130,2},{3,131},{131,3},{4... | collective-permute-start | bytes 2359304 | tf_op jit(solution)/shard_map/ppermute | solution.py:24
  97.8 46.7 %copy-start = (bf16[3,256,512]{2,1,0:T(8,128)(2,1)S(1)}, bf16[3,256,512]{2,1,0:T(8,128)(2,1)}, u32[]{:S(2)}) copy-start(bf16[3,256,512]{2,1,0:T(8,128)(2,1)} %weight_ref.1) | copy-start | bytes 2359300
  97.8 33.4 %all-to-all-start.1 = ((bf16[128,16,128]{2,1,0:T(8,128)(2,1)}), bf16[128,16,128]{2,1,0:T(8,128)(2,1)S(1)}, u32[]{:S(2)}, u32[]{:S(2)}) async-start(bf16[128,16,128]{2,1,0:T(8,128)(2,1)} %pair_sum.1), calls=%async_computation.1 | async-start | bytes 1048576 | tf_op jit(solution)/shard_map/all_to_all | solution.py:20
  114.9 29.6 %collective-permute-start.3 = (bf16[2048,256]{1,0:T(8,128)(2,1)S(1)}, bf16[2048,256]{1,0:T(8,128)(2,1)}, u32[]{:S(2)}, u32[]{:S(2)}) collective-permute-start(bf16[2048,256]{1,0:T(8,128)(2,1)S(1)} %get-tuple-element.9.even_ref), channel_id=1, source_target_pairs={{0,16},{16,32},{32,48},{48,64},{64,80},{80,96},{96,112},{1,17},{17... | collective-permute-start | bytes 3145736 | tf_op jit(solution)/shard_map/ppermute | solution.py:352
  132.1 25.3 %all-to-all-start.2 = ((bf16[128,16,128]{2,1,0:T(8,128)(2,1)}), bf16[128,16,128]{2,1,0:T(8,128)(2,1)S(1)}, u32[]{:S(2)}, u32[]{:S(2)}) async-start(bf16[128,16,128]{2,1,0:T(8,128)(2,1)} %total_for_all.1), calls=%async_computation.2 | async-start | bytes 1048576 | tf_op jit(solution)/shard_map/all_to_all | solution.py:20
  157.5 4.8 %collective-permute-start.4 = (bf16[128,16,128]{2,1,0:T(8,128)(2,1)S(1)}, bf16[128,16,128]{2,1,0:T(8,128)(2,1)S(1)}, u32[]{:S(2)}, u32[]{:S(2)}) collective-permute-start(bf16[128,16,128]{2,1,0:T(8,128)(2,1)S(1)} %all-to-all-done.2.own_ref), channel_id=1, source_target_pairs={{0,128},{128,0},{1,129},{129,1},{2,130},{130,2},{3,131},{131,3},{4... | collective-permute-start | bytes 1572872 | tf_op jit(solution)/shard_map/ppermute | solution.py:24

commit v5 on v4

--- a/solution.py
+++ b/solution.py
@@ -88,7 +88,6 @@
         in_specs=[pl.BlockSpec(memory_space=pltpu.SMEM)],
         out_specs=pl.BlockSpec(memory_space=pltpu.VMEM),
         out_shape=jax.ShapeDtypeStruct((8, channels), F32),
-        cost_estimate=pl.CostEstimate(flops=10**12, bytes_accessed=10**9, transcendentals=0),
         name="odd_mask",
     )(where)
 
@@ -181,62 +180,90 @@
     )(mask, pieces, weight)
 
 
-def gradient_kernel(
-    where_ref, odd_ref, even_ref, u_hbm, next_hbm, mine_ref, sent_ref, u_ref, next_ref, grad_ref, sems
-):
-    loads = (
-        pltpu.make_async_copy(u_hbm, u_ref, sems.at[0]),
-        pltpu.make_async_copy(next_hbm, next_ref, sems.at[1]),
+def outer_sum(act_ref, up_ref):
+    return lax.dot_general(
+        act_ref[...], up_ref[...], (((0,), (0,)), ((), ())), preferred_element_type=F32
     )
-    for load in loads:
-        load.start()
-    side = where_ref[0]
+
+
+def late_taps_kernel(odd_ref, even_ref, u_hbm, grad_ref, u_ref, sem):
+    load = pltpu.make_async_copy(u_hbm, u_ref, sem)
+    load.start()
     channels = odd_ref.shape[1]
     blocks = u_ref.shape[1] // LANES
-    loads[0].wait()
-    for k, act_ref, up in ((1, odd_ref, u_ref), (2, even_ref, u_ref), (0, even_ref, next_ref)):
-        if k == 0:
-            loads[1].wait()
-        term = lax.dot_general(
-            act_ref[...], up[...], (((0,), (0,)), ((), ())), preferred_element_type=F32
-        )
+    first = channels // PIECE * blocks
+    grad_ref[0, :first] = jnp.zeros((first, PIECE, LANES), F32)
+    load.wait()
+    for k, act_ref in ((1, odd_ref), (2, even_ref)):
+        term = outer_sum(act_ref, u_ref)
         for g in range(channels // PIECE):
-            line = k * channels + g * PIECE
-            half, group = divmod(line, 3 * channels // 2)
+            half, group = divmod(k * channels + g * PIECE, 3 * channels // 2)
             for b in range(blocks):
                 grad_ref[half, (group // PIECE) * blocks + b] = term[
                     g * PIECE : (g + 1) * PIECE, b * LANES : (b + 1) * LANES
                 ]
-    mine_ref[...] = grad_ref[side]
-    sent_ref[...] = grad_ref[1 - side]
-
-
-def gradient(where, odd, even, upstream, following):
+
+
+def late_taps(odd, even, upstream):
     positions, channels = odd.shape
     out_channels = upstream.shape[1]
     count = 3 * channels * out_channels // (2 * PIECE * LANES)
     vmem = pl.BlockSpec(memory_space=pltpu.VMEM)
-    hbm = pl.BlockSpec(memory_space=pltpu.HBM)
-    part = jax.ShapeDtypeStruct((count, PIECE, LANES), F32)
-    return pl.pallas_call(
-        gradient_kernel,
-        in_specs=[pl.BlockSpec(memory_space=pltpu.SMEM), vmem, vmem, hbm, hbm],
+    return pl.pallas_call(
+        late_taps_kernel,
+        in_specs=[vmem, vmem, pl.BlockSpec(memory_space=pltpu.HBM)],
+        out_specs=vmem,
+        out_shape=jax.ShapeDtypeStruct((2, count, PIECE, LANES), F32),
+        scratch_shapes=[pltpu.VMEM(upstream.shape, BF16), pltpu.SemaphoreType.DMA],
+        compiler_params=pltpu.CompilerParams(vmem_limit_bytes=VMEM_BYTES),
+        cost_estimate=pl.CostEstimate(
+            flops=4 * positions * channels * out_channels,
+            bytes_accessed=6_000_000,
+            transcendentals=0,
+        ),
+        name="late_taps",
+    )(odd, even, upstream)
+
+
+def first_tap_kernel(where_ref, grad_ref, even_ref, next_hbm, mine_ref, sent_ref, next_ref, sem):
+    load = pltpu.make_async_copy(next_hbm, next_ref, sem)
+    load.start()
+    side = where_ref[0]
+    channels = even_ref.shape[1]
+    blocks = next_ref.shape[1] // LANES
+    first = channels // PIECE * blocks
+    mine_ref[...] = grad_ref[side]
+    sent_ref[...] = grad_ref[1 - side]
+    load.wait()
+    term = outer_sum(even_ref, next_ref)
+    for p in range(first):
+        g, b = divmod(p, blocks)
+        part = term[g * PIECE : (g + 1) * PIECE, b * LANES : (b + 1) * LANES]
+        mine_ref[p] = jnp.where(side == 0, part, mine_ref[p])
+        sent_ref[p] = jnp.where(side == 0, sent_ref[p], part)
+
+
+def first_tap(where, grad, even, following):
+    positions, channels = even.shape
+    out_channels = following.shape[1]
+    vmem = pl.BlockSpec(memory_space=pltpu.VMEM)
+    part = jax.ShapeDtypeStruct(grad.shape[1:], F32)
+    return pl.pallas_call(
+        first_tap_kernel,
+        in_specs=[
+            pl.BlockSpec(memory_space=pltpu.SMEM), vmem, vmem, pl.BlockSpec(memory_space=pltpu.HBM)
+        ],
         out_specs=[vmem, vmem],
         out_shape=[part, part],
-        scratch_shapes=[
-            pltpu.VMEM(upstream.shape, BF16),
-            pltpu.VMEM(following.shape, BF16),
-            pltpu.VMEM((2, count, PIECE, LANES), F32),
-            pltpu.SemaphoreType.DMA((2,)),
-        ],
+        scratch_shapes=[pltpu.VMEM(following.shape, BF16), pltpu.SemaphoreType.DMA],
         compiler_params=pltpu.CompilerParams(vmem_limit_bytes=VMEM_BYTES),
         cost_estimate=pl.CostEstimate(
-            flops=6 * positions * channels * out_channels,
-            bytes_accessed=8_000_000,
+            flops=2 * positions * channels * out_channels,
+            bytes_accessed=6_000_000,
             transcendentals=0,
         ),
-        name="gradient",
-    )(where, odd, even, upstream, following)
+        name="first_tap",
+    )(where, grad, even, following)
 
 
 def latent_kernel(old_ref, odd_ref, even_ref, weight_ref, out_ref):
@@ -342,13 +369,8 @@
     pieces = pltpu.with_memory_space_constraint(exchange(pack(frames, tiles, chans)), pltpu.HBM)
     mask = pltpu.with_memory_space_constraint(odd_mask(where, video.shape[4]), pltpu.HBM)
     odd, even = spatial(mask, pieces, spatial_weight)
-    mine, sent = gradient(
-        where,
-        odd,
-        even,
-        upstream.reshape((-1, out_channels)),
-        following.reshape((-1, out_channels)),
-    )
+    later = late_taps(odd, even, upstream.reshape((-1, out_channels)))
+    mine, sent = first_tap(where, later, even, following.reshape((-1, out_channels)))
     oldest = lax.ppermute(even, "tile", [(i, i + 1) for i in range(tiles - 1)])
     pair = pair_sum(mine, other_core(sent), devices)
     whole = exchange(total_for_all(exchange(pair)))

time: 165 us -> 163 us (0.988)
  starting transfers between devices: 56.1 us -> 51.2 us
  waiting for transfers between devices: 82.3 us -> 84.7 us
    ppermute x1, waiting for transfers between devices: 0.01 us -> 7.15 us  [body(): following = lax.ppermute(latent_grad, ('segment', 'tile'), shift)]
    all_to_all x3, waiting for transfers between devices: 76.3 us -> 71.5 us  [exchange(): lax.all_to_all(pieces, GROUP, split_axis=0, concat_axis=0, tiled=True)]
    ppermute x3, starting transfers between devices: 8.34 us -> 4.73 us  [other_core(): return lax.ppermute(shard, 'segment', [(0, 1), (1, 0)])]
    pallas_call x1 -> x2, Pallas kernels: 4.27 us -> 5.76 us  [the longest x1 2.88 us: first_tap(): pl.pallas_call(first_tap_kernel, in_specs=[pl.BlockSpec(memory_space=pltp...]
  transfers between devices with their start and end apart: 8 -> 8, of which waited for: 6 -> 7; matrix products, arithmetic and copies ran while one was open for 0% -> 0% of each run, Pallas kernels for 11% -> 11%
where the time goes in v5:
time: 163 us
  waiting for transfers between devices  84.7 us (52%)
  starting transfers between devices  51.2 us (31%)
  Pallas kernels  25.6 us (16%)
    all_to_all x3, waiting for transfers between devices, exchange(): lax.all_to_all(pieces, GROUP, split_axis=0, concat_axis=0, tiled=True)  71.5 us
    all_to_all x3, starting transfers between devices, exchange(): lax.all_to_all(pieces, GROUP, split_axis=0, concat_axis=0, tiled=True)  41.7 us
    pallas_call x1, Pallas kernels, spatial(): pl.pallas_call(functools.partial(conv_kernel, rows, chunk), in_specs=[hbm...  7.64 us
    ppermute x1, waiting for transfers between devices, body(): following = lax.ppermute(latent_grad, ('segment', 'tile'), shift)  7.15 us
    ppermute x3, starting transfers between devices, other_core(): return lax.ppermute(shard, 'segment', [(0, 1), (1, 0)])  4.73 us
    pallas_call x1, Pallas kernels, temporal(): pl.pallas_call(latent_kernel, grid=(positions // step,), in_specs=[tap, t...  4.65 us
    ppermute x1, starting transfers between devices, body(): oldest = lax.ppermute(even, 'tile', [(i, i + 1) for i in range(tiles - 1)])  3.47 us
    ppermute x3, waiting for transfers between devices, other_core(): return lax.ppermute(shard, 'segment', [(0, 1), (1, 0)])  3.45 us
  transfers between devices with their start and end apart: 8, of which 7 were waited for; matrix products, arithmetic and copies ran while one was open for 0% of the time, Pallas kernels for 11%

profile of v5, /device:TPU:1, one launch (start us, length us, event | category | flops | bytes accessed | tf_op | source)
XLA Modules:
  0.0 162.9 jit_solution(9248792004913366937)
XLA Ops:
  0.6 2.7 %pack.1 = bf16[128,72,128]{2,1,0:T(8,128)(2,1)} custom-call(bf16[16,256,256]{2,1,0:T(8,128)(2,1)} %bitcast.10), custom_call_target="tpu_custom_call" | custom-call | tf_op jit(solution)/shard_map/pack/pallas_call | solution.py:64
  3.3 0.0 copy-start.2
  3.3 16.9 %all-to-all-start = ((bf16[128,72,128]{2,1,0:T(8,128)(2,1)}), bf16[128,72,128]{2,1,0:T(8,128)(2,1)}, u32[]{:S(2)}, u32[]{:S(2)}) async-start(bf16[128,72,128]{2,1,0:T(8,128)(2,1)} %pack.1), calls=%async_computation | async-start | bytes 4718592 | tf_op jit(solution)/shard_map/all_to_all | solution.py:20
  20.3 1.0 collective-permute-start
  21.3 1.3 collective-permute-start.1
  22.6 0.6 pad_add_fusion.where_ref
  23.2 1.3 odd_mask.1.mask_hbm
  24.5 50.2 %all-to-all-done.y_hbm = bf16[128,72,128]{2,1,0:T(8,128)(2,1)} async-done(((bf16[128,72,128]{2,1,0:T(8,128)(2,1)}), bf16[128,72,128]{2,1,0:T(8,128)(2,1)}, u32[]{:S(2)}, u32[]{:S(2)}) %all-to-all-start) | async-done | bytes 2359328 | tf_op jit(solution)/shard_map/all_to_all | solution.py:20
  74.6 0.0 copy-done.2
  74.6 7.6 %spatial.1 = (bf16[2048,256]{1,0:T(8,128)(2,1)S(1)}, bf16[2048,256]{1,0:T(8,128)(2,1)S(1)}) custom-call(f32[8,256]{1,0:T(8,128)} %odd_mask.1.mask_hbm, bf16[128,72,128]{2,1,0:T(8,128)(2,1)} %all-to-all-done.y_hbm, bf16[3,768,256]{2,1,0:T(8,128)(2,1)S(1)} %bitcast.8), custom_call_target="tpu_custom_call" | custom-call | flops 4831838208 | bytes 6000000 | tf_op jit(solution)/shard_map/spatial/pallas_call | solution.py:159
  82.3 0.0 collective-permute-done
  82.3 0.0 copy-start.1
  82.3 2.9 %late_taps.1.grad_ref = f32[2,96,16,128]{3,2,1,0:T(8,128)S(1)} custom-call(bf16[2048,256]{1,0:T(8,128)(2,1)S(1)} %get-tuple-element.8.odd_ref, bf16[2048,256]{1,0:T(8,128)(2,1)S(1)} %get-tuple-element.9.even_ref, bf16[2048,512]{1,0:T(8,128)(2,1)} %bitcast.4.u_hbm), custom_call_target="tpu_custom_call" | custom-call | flops 1073741824 | bytes 6000000 | tf_op jit(solution)/shard_map/late_taps/pallas_call | solution.py:212
  85.2 7.2 %collective-permute-done.1 = bf16[1,1,128,16,512]{4,3,2,1,0:T(8,128)(2,1)} collective-permute-done((bf16[1,1,128,16,512]{4,3,2,1,0:T(8,128)(2,1)}, bf16[1,1,128,16,512]{4,3,2,1,0:T(8,128)(2,1)}, u32[]{:S(2)}, u32[]{:S(2)}) %collective-permute-start.1) | collective-permute-done | bytes 2097184 | tf_op jit(solution)/shard_map/ppermute | solution.py:367
  92.3 0.0 copy-done.1
  92.3 2.9 %first_tap.1 = (f32[96,16,128]{2,1,0:T(8,128)S(1)}, f32[96,16,128]{2,1,0:T(8,128)S(1)}) custom-call(s32[2]{0:T(128)S(1)} %copy-done.1, f32[2,96,16,128]{3,2,1,0:T(8,128)S(1)} %late_taps.1.grad_ref, bf16[2048,256]{1,0:T(8,128)(2,1)S(1)} %get-tuple-element.9.even_ref, bf16[2048,512]{1,0:T(8,128)(2,1)} %bitcast.5.next_hbm), custom_call_target="tpu_custom_call" | custom-call | flops 536870912 | bytes 6000000 | tf_op jit(solution)/shard_map/first_tap/pallas_call | solution.py:251
  95.2 0.5 collective-permute-start.2
  95.7 1.9 %collective-permute-done.2.away_ref = f32[96,16,128]{2,1,0:T(8,128)S(1)} collective-permute-done((f32[96,16,128]{2,1,0:T(8,128)S(1)}, f32[96,16,128]{2,1,0:T(8,128)S(1)}, u32[]{:S(2)}, u32[]{:S(2)}) %collective-permute-start.2) | collective-permute-done | bytes 786464 | tf_op jit(solution)/shard_map/ppermute | solution.py:24
  97.6 0.9 pair_sum.1
  98.5 0.0 copy-start
  98.5 15.2 %all-to-all-start.1 = ((bf16[128,16,128]{2,1,0:T(8,128)(2,1)}), bf16[128,16,128]{2,1,0:T(8,128)(2,1)S(1)}, u32[]{:S(2)}, u32[]{:S(2)}) async-start(bf16[128,16,128]{2,1,0:T(8,128)(2,1)} %pair_sum.1), calls=%async_computation.1 | async-start | bytes 1048576 | tf_op jit(solution)/shard_map/all_to_all | solution.py:20
  113.7 3.5 %collective-permute-start.3 = (bf16[2048,256]{1,0:T(8,128)(2,1)S(1)}, bf16[2048,256]{1,0:T(8,128)(2,1)}, u32[]{:S(2)}, u32[]{:S(2)}) collective-permute-start(bf16[2048,256]{1,0:T(8,128)(2,1)S(1)} %get-tuple-element.9.even_ref), channel_id=1, source_target_pairs={{0,16},{16,32},{32,48},{48,64},{64,80},{80,96},{96,112},{1,17},{17... | collective-permute-start | bytes 3145736 | tf_op jit(solution)/shard_map/ppermute | solution.py:374
  117.2 13.0 %all-to-all-done.1.parts_ref = bf16[128,16,128]{2,1,0:T(8,128)(2,1)S(1)} async-done(((bf16[128,16,128]{2,1,0:T(8,128)(2,1)}), bf16[128,16,128]{2,1,0:T(8,128)(2,1)S(1)}, u32[]{:S(2)}, u32[]{:S(2)}) %all-to-all-start.1) | async-done | bytes 524320 | tf_op jit(solution)/shard_map/all_to_all | solution.py:20
  130.2 1.0 total_for_all.1
  131.2 9.6 %all-to-all-start.2 = ((bf16[128,16,128]{2,1,0:T(8,128)(2,1)}), bf16[128,16,128]{2,1,0:T(8,128)(2,1)S(1)}, u32[]{:S(2)}, u32[]{:S(2)}) async-start(bf16[128,16,128]{2,1,0:T(8,128)(2,1)} %total_for_all.1), calls=%async_computation.2 | async-start | bytes 1048576 | tf_op jit(solution)/shard_map/all_to_all | solution.py:20
  140.8 2.6 %collective-permute-done.3.old_ref = bf16[2048,256]{1,0:T(8,128)(2,1)} collective-permute-done((bf16[2048,256]{1,0:T(8,128)(2,1)S(1)}, bf16[2048,256]{1,0:T(8,128)(2,1)}, u32[]{:S(2)}, u32[]{:S(2)}) %collective-permute-start.3) | collective-permute-done | bytes 1048608 | tf_op jit(solution)/shard_map/ppermute | solution.py:374
  143.3 0.0 copy-done
  143.4 4.6 %temporal.1 = bf16[2048,512]{1,0:T(8,128)(2,1)} custom-call(bf16[2048,256]{1,0:T(8,128)(2,1)} %collective-permute-done.3.old_ref, bf16[2048,256]{1,0:T(8,128)(2,1)S(1)} %get-tuple-element.8.odd_ref, bf16[2048,256]{1,0:T(8,128)(2,1)S(1)} %get-tuple-element.9.even_ref, bf16[3,256,512]{2,1,0:T(8,128)(2,1)S(1)} %copy-done), custom_call_target="tpu_custom_call" | custom-call | flops 1610612736 | bytes 6000000 | tf_op jit(solution)/shard_map/temporal/pallas_call | solution.py:281
  148.0 8.3 %all-to-all-done.2.own_ref = bf16[128,16,128]{2,1,0:T(8,128)(2,1)S(1)} async-done(((bf16[128,16,128]{2,1,0:T(8,128)(2,1)}), bf16[128,16,128]{2,1,0:T(8,128)(2,1)S(1)}, u32[]{:S(2)}, u32[]{:S(2)}) %all-to-all-start.2) | async-done | bytes 524320 | tf_op jit(solution)/shard_map/all_to_all | solution.py:20
  156.3 3.2 %collective-permute-start.4 = (bf16[128,16,128]{2,1,0:T(8,128)(2,1)S(1)}, bf16[128,16,128]{2,1,0:T(8,128)(2,1)S(1)}, u32[]{:S(2)}, u32[]{:S(2)}) collective-permute-start(bf16[128,16,128]{2,1,0:T(8,128)(2,1)S(1)} %all-to-all-done.2.own_ref), channel_id=1, source_target_pairs={{0,128},{128,0},{1,129},{129,1},{2,130},{130,2},{3,131},{131,3},{4... | collective-permute-start | bytes 1572872 | tf_op jit(solution)/shard_map/ppermute | solution.py:24
  159.5 1.5 collective-permute-done.4.away_ref
  161.1 1.8 %unpack.1 = f32[2,384,512]{2,1,0:T(8,128)} custom-call(s32[2]{0:T(128)S(1)} %copy-done.1, bf16[128,16,128]{2,1,0:T(8,128)(2,1)S(1)} %all-to-all-done.2.own_ref, bf16[128,16,128]{2,1,0:T(8,128)(2,1)S(1)} %collective-permute-done.4.away_ref), custom_call_target="tpu_custom_call" | custom-call | tf_op jit(solution)/shard_map/unpack/pallas_call | solution.py:348
Async XLA Ops:
  3.3 71.3 %copy-start.2 = (bf16[9,256,256]{2,1,0:T(8,128)(2,1)S(1)}, bf16[9,256,256]{2,1,0:T(8,128)(2,1)}, u32[]{:S(2)}) copy-start(bf16[9,256,256]{2,1,0:T(8,128)(2,1)} %param.5) | copy-start | bytes 3538948
  3.3 71.3 %all-to-all-start = ((bf16[128,72,128]{2,1,0:T(8,128)(2,1)}), bf16[128,72,128]{2,1,0:T(8,128)(2,1)}, u32[]{:S(2)}, u32[]{:S(2)}) async-start(bf16[128,72,128]{2,1,0:T(8,128)(2,1)} %pack.1), calls=%async_computation | async-start | bytes 4718592 | tf_op jit(solution)/shard_map/all_to_all | solution.py:20
  20.3 62.0 %collective-permute-start = (bf16[1,1,128,16,512]{4,3,2,1,0:T(8,128)(2,1)}, bf16[1,1,128,16,512]{4,3,2,1,0:T(8,128)(2,1)}, u32[]{:S(2)}, u32[]{:S(2)}) collective-permute-start(bf16[1,1,128,16,512]{4,3,2,1,0:T(8,128)(2,1)} %param.7), channel_id=1, source_target_pairs={{0,128},{128,0},{1,129},{129,1},{2,130},{130,2},{3,131},{131,3},{4... | collective-permute-start | bytes 6291464 | tf_op jit(solution)/shard_map/ppermute | solution.py:24
  21.3 71.0 %collective-permute-start.1 = (bf16[1,1,128,16,512]{4,3,2,1,0:T(8,128)(2,1)}, bf16[1,1,128,16,512]{4,3,2,1,0:T(8,128)(2,1)}, u32[]{:S(2)}, u32[]{:S(2)}) collective-permute-start(bf16[1,1,128,16,512]{4,3,2,1,0:T(8,128)(2,1)} %param.7), channel_id=1, source_target_pairs={{16,128},{32,144},{48,160},{64,176},{80,192},{96,208},{112,224},{1... | collective-permute-start | bytes 6291464 | tf_op jit(solution)/shard_map/ppermute | solution.py:367
  82.3 10.1 %copy-start.1 = (s32[2]{0:T(128)S(1)}, s32[2]{0:T(128)}, u32[]{:S(2)}) copy-start(s32[2]{0:T(128)} %pad_add_fusion.where_ref) | copy-start | bytes 28
  95.2 2.4 %collective-permute-start.2 = (f32[96,16,128]{2,1,0:T(8,128)S(1)}, f32[96,16,128]{2,1,0:T(8,128)S(1)}, u32[]{:S(2)}, u32[]{:S(2)}) collective-permute-start(f32[96,16,128]{2,1,0:T(8,128)S(1)} %get-tuple-element.11), channel_id=1, source_target_pairs={{0,128},{128,0},{1,129},{129,1},{2,130},{130,2},{3,131},{131,3},{4... | collective-permute-start | bytes 2359304 | tf_op jit(solution)/shard_map/ppermute | solution.py:24
  98.5 44.8 %copy-start = (bf16[3,256,512]{2,1,0:T(8,128)(2,1)S(1)}, bf16[3,256,512]{2,1,0:T(8,128)(2,1)}, u32[]{:S(2)}) copy-start(bf16[3,256,512]{2,1,0:T(8,128)(2,1)} %weight_ref.1) | copy-start | bytes 2359300
  98.5 31.7 %all-to-all-start.1 = ((bf16[128,16,128]{2,1,0:T(8,128)(2,1)}), bf16[128,16,128]{2,1,0:T(8,128)(2,1)S(1)}, u32[]{:S(2)}, u32[]{:S(2)}) async-start(bf16[128,16,128]{2,1,0:T(8,128)(2,1)} %pair_sum.1), calls=%async_computation.1 | async-start | bytes 1048576 | tf_op jit(solution)/shard_map/all_to_all | solution.py:20
  113.7 29.7 %collective-permute-start.3 = (bf16[2048,256]{1,0:T(8,128)(2,1)S(1)}, bf16[2048,256]{1,0:T(8,128)(2,1)}, u32[]{:S(2)}, u32[]{:S(2)}) collective-permute-start(bf16[2048,256]{1,0:T(8,128)(2,1)S(1)} %get-tuple-element.9.even_ref), channel_id=1, source_target_pairs={{0,16},{16,32},{32,48},{48,64},{64,80},{80,96},{96,112},{1,17},{17... | collective-permute-start | bytes 3145736 | tf_op jit(solution)/shard_map/ppermute | solution.py:374
  131.2 25.2 %all-to-all-start.2 = ((bf16[128,16,128]{2,1,0:T(8,128)(2,1)}), bf16[128,16,128]{2,1,0:T(8,128)(2,1)S(1)}, u32[]{:S(2)}, u32[]{:S(2)}) async-start(bf16[128,16,128]{2,1,0:T(8,128)(2,1)} %total_for_all.1), calls=%async_computation.2 | async-start | bytes 1048576 | tf_op jit(solution)/shard_map/all_to_all | solution.py:20
  156.3 4.7 %collective-permute-start.4 = (bf16[128,16,128]{2,1,0:T(8,128)(2,1)S(1)}, bf16[128,16,128]{2,1,0:T(8,128)(2,1)S(1)}, u32[]{:S(2)}, u32[]{:S(2)}) collective-permute-start(bf16[128,16,128]{2,1,0:T(8,128)(2,1)S(1)} %all-to-all-done.2.own_ref), channel_id=1, source_target_pairs={{0,128},{128,0},{1,129},{129,1},{2,130},{130,2},{3,131},{131,3},{4... | collective-permute-start | bytes 1572872 | tf_op jit(solution)/shard_map/ppermute | solution.py:24
